TPU v7x, 1024 devices: a whole 8x8x8 slice. The times are simulated.
1024 devices in a mesh: ctx: 128 (over z_lo, y, x), tp: 8 (over z_hi, core).
Axes of the slice: x: 8, y: 8, z: 8 (z_hi: 4, z_lo: 2; z = z_hi * 2 + z_lo), core: 2. Of those that a mesh axis runs over, the one named last changes fastest.
Arguments:
- value_path: bfloat16 [16384, 8192], P('ctx', 'tp'), may hold values from -6 to 6
- key_se: bfloat16 [16384, 8192], P('ctx', 'tp'), may hold values from -6 to 6
- query_se: bfloat16 [16384, 8192], P('ctx', 'tp'), may hold values from -60 to 60
- key_mr: bfloat16 [16384, 8192], P('ctx', 'tp'), may hold values from -6 to 6
- query_mr: bfloat16 [16384, 8192], P('ctx', 'tp'), may hold values from -6 to 6
- out_grad: bfloat16 [16384, 8192], P('ctx', 'tp'), may hold values from -6 to 6
- norm_gain: bfloat16 [8192], P('tp'), may hold values from 0.099609375 to 1.8984375
- filter_se: bfloat16 [7, 8192], P(None, 'tp'), may hold values from -2 to 2
- filter_mr: bfloat16 [128, 8192], P(None, 'tp'), may hold values from -0.5 to 0.5
Outputs:
- grad_value: bfloat16 [16384, 8192], P('ctx', 'tp')
- grad_query_se: bfloat16 [16384, 8192], P('ctx', 'tp')
- grad_key_se: bfloat16 [16384, 8192], P('ctx', 'tp')
- grad_query_mr: bfloat16 [16384, 8192], P('ctx', 'tp')
- grad_key_mr: bfloat16 [16384, 8192], P('ctx', 'tp')
- grad_filter_se: float32 [7, 8192], P(None, 'tp')
- grad_filter_mr: float32 [128, 8192], P(None, 'tp')
- grad_gain: float32 [8192], P('tp')
All inputs are finite; a program needn't handle non-finite values.
Results may differ from a plain program's by a relative error of at most 0.015.
Values may be sent and summed in bfloat16 or wider, within the bound.
No kernel may reach another device: no remote copies, remote signals or barrier semaphores. Data moves between devices by JAX's collectives and lax.ppermute only.
A program may use at most 32 MiB of HBM per device.

v0:
```python
import jax
import jax.numpy as jnp
from jax import lax
from jax.sharding import PartitionSpec as P

D = 8192


def shifted(block, axis, distance):
    devices = range(lax.axis_size(axis))
    route = [(i - distance, i) for i in devices if i - distance in devices]
    return lax.ppermute(block, axis, route)


def depthwise(lhs, kernel):
    out = lax.conv_general_dilated(
        lhs[None],
        kernel[:, None, :],
        (1,),
        "VALID",
        dimension_numbers=("NWC", "WIO", "NWC"),
        feature_group_count=lhs.shape[1],
        preferred_element_type=jnp.float32,
    )
    return out[0]


def from_left(block, width):
    return shifted(block[block.shape[0] - width :], "ctx", 1)


def from_right(block, width):
    return shifted(block[:width], "ctx", -1)


def token_total(partial_sum):
    return lax.psum(partial_sum, "tp")


def shards(
    value_path, key_se, query_se, key_mr, query_mr, out_grad, norm_gain, filter_se, filter_mr
):
    f32 = jnp.float32
    bf16 = jnp.bfloat16
    se_taps = filter_se.shape[0]
    mr_taps = filter_mr.shape[0]
    prod_se = (key_se.astype(f32) * value_path.astype(f32)).astype(bf16)
    grad_conv_mr = (out_grad.astype(f32) * query_mr.astype(f32)).astype(bf16)
    rim_se = from_left(prod_se, se_taps - 1)
    rim_grad_mr = from_right(grad_conv_mr, mr_taps - 1)
    pad_se = jnp.concatenate([rim_se, prod_se], axis=0)
    conv_se = depthwise(pad_se, filter_se[::-1])
    mixed_se = query_se.astype(f32) * conv_se
    grad_prod_mr = depthwise(jnp.concatenate([grad_conv_mr, rim_grad_mr], axis=0), filter_mr)
    gain = norm_gain.astype(f32)
    grad_normed = grad_prod_mr * key_mr.astype(f32)
    scaled = grad_normed * gain
    square_part = jnp.sum(mixed_se * mixed_se, axis=1, keepdims=True)
    dot_part = jnp.sum(scaled * mixed_se, axis=1, keepdims=True)
    square_total = token_total(square_part)
    inv_rms = lax.rsqrt(square_total / D + 1e-06)
    normed = (mixed_se * inv_rms * gain).astype(bf16)
    prod_mr = (key_mr.astype(f32) * normed.astype(f32)).astype(bf16)
    rim_mr = from_left(prod_mr, mr_taps - 1)
    pad_mr = jnp.concatenate([rim_mr, prod_mr], axis=0)
    conv_mr = depthwise(pad_mr, filter_mr[::-1])
    grad_query_mr = (out_grad.astype(f32) * conv_mr).astype(bf16)
    grad_key_mr = (grad_prod_mr * normed.astype(f32)).astype(bf16)
    local_filter_mr = depthwise(pad_mr, grad_conv_mr)[::-1]
    grad_filter_mr = lax.psum(local_filter_mr, "ctx")
    local_gain = jnp.sum(grad_normed * mixed_se * inv_rms, axis=0)
    dot_sum = token_total(dot_part)
    grad_mixed = inv_rms * scaled - mixed_se * (inv_rms * inv_rms * inv_rms) * dot_sum / D
    grad_query_se = (grad_mixed * conv_se).astype(bf16)
    grad_conv_se = (grad_mixed * query_se.astype(f32)).astype(bf16)
    rim_grad_se = from_right(grad_conv_se, se_taps - 1)
    grad_prod_se = depthwise(jnp.concatenate([grad_conv_se, rim_grad_se], axis=0), filter_se)
    grad_key_se = (grad_prod_se * value_path.astype(f32)).astype(bf16)
    grad_value = (grad_prod_se * key_se.astype(f32)).astype(bf16)
    local_filter_se = depthwise(pad_se, grad_conv_se)[::-1]
    grad_filter_se, grad_gain = lax.psum((local_filter_se, local_gain), "ctx")
    return (
        grad_value,
        grad_query_se,
        grad_key_se,
        grad_query_mr,
        grad_key_mr,
        grad_filter_se,
        grad_filter_mr,
        grad_gain,
    )


def solution(mesh):
    placed = (
        P("ctx", "tp"),
        P("ctx", "tp"),
        P("ctx", "tp"),
        P("ctx", "tp"),
        P("ctx", "tp"),
        P("ctx", "tp"),
        P("tp"),
        P(None, "tp"),
        P(None, "tp"),
    )
    return jax.shard_map(
        shards,
        mesh=mesh,
        in_specs=placed,
        out_specs=(
            P("ctx", "tp"),
            P("ctx", "tp"),
            P("ctx", "tp"),
            P("ctx", "tp"),
            P("ctx", "tp"),
            P(None, "tp"),
            P(None, "tp"),
            P("tp"),
        ),
        check_vma=False,
    )
```

profile of v0, /device:TPU:128, one launch (start us, length us, event | category | flops | bytes accessed | tf_op | source)
XLA Modules:
  0.0 1795.8 jit_solution(16690547387549673512)
XLA Ops:
  7.2 0.0 copy-start.5
  7.2 0.0 copy-start.2
  7.2 0.0 all-reduce.3.cloned.1.call-start
  7.2 1.1 fusion.12
  8.4 0.0 copy-start.8
  8.4 0.0 copy-start.6
  8.4 3.5 collective-permute-start
  12.0 0.0 copy-done.5
  12.0 0.0 copy-done.2
  12.0 0.1 fusion.14
  12.1 0.0 copy-start.9
  12.1 6.7 collective-permute-start.1
  18.7 0.0 copy-done.8
  18.7 0.2 rev.12
  19.0 0.0 copy-done.9
  19.0 2.6 rev.13
  21.6 0.0 collective-permute-done
  21.6 0.1 maximum_bitcast_fusion.2
  21.7 0.1 reshape.20
  21.9 0.2 copy.28
  22.0 0.0 copy-start.10
  22.1 0.6 copy-done.10
  22.7 0.3 convolution_select_fusion.1
  23.0 0.3 copy.30
  23.4 0.0 copy-start.3
  23.4 0.1 reshape.24
  23.5 0.9 copy-done.3
  24.3 0.2 multiply_reduce_fusion.2
  24.5 26.7 %psum.35 = f32[128,1]{0,1:T(1,128)S(1)} all-reduce(f32[128,1]{0,1:T(1,128)S(1)} %bitcast.69), channel_id=1, replica_groups=mesh['ctx'=128,'tp'=8] {'tp'}, use_global_device_ids=true, to_apply=%region_1.0 | all-reduce | flops 128 | bytes 1024 | tf_op jit(solution)/shard_map/psum | solution.py:37
  51.2 0.0 collective-permute-done.1
  51.2 0.0 copy-start.4
  51.2 7.3 fusion
  58.6 0.0 copy-done.4
  58.6 1.0 multiply_reduce_fusion
  59.6 14.2 psum.36
  73.8 1.0 multiply_convert_fusion.1
  74.8 1.1 fusion.8
  76.0 0.2 rev.14
  76.2 3.3 collective-permute-start.2
  79.5 0.1 slice.27
  79.6 2.5 collective-permute-start.3
  82.1 610.3 %all-reduce = (f32[7,1024]{1,0:T(8,128)}, f32[1024]{0:T(1024)}) all-reduce(f32[7,1024]{1,0:T(8,128)S(1)} %rev.14, f32[1024]{0:T(1024)S(1)} %get-tuple-element.8), channel_id=1, replica_groups=mesh['ctx'=128,'tp'=8] {'ctx'}, use_global_device_ids=true, to_apply=%region_4.0 | all-reduce | flops 8192 | bytes 65536 | tf_op jit(solution)/shard_map/psum | solution.py:81
  692.5 0.0 collective-permute-done.2
  692.5 0.1 reshape.27
  692.6 0.2 copy.34
  692.8 0.3 convolution_select_fusion
  693.2 0.3 copy.36
  693.5 0.0 copy-start
  693.5 0.0 copy-start.1
  693.5 0.1 reshape.31
  693.6 0.8 copy-done
  694.5 0.1 copy-done.1
  694.5 0.9 fusion.13
  695.5 0.0 collective-permute-done.3
  695.5 0.1 maximum_bitcast_fusion.1
  695.6 7.3 fusion.2
  702.9 0.1 copy.82
  703.0 2.6 rev.15
  705.6 0.0 all-reduce.3.cloned.1.call-update
  705.7 0.9 copy-done.7
  706.6 7.3 fusion.4
  713.9 0.8 fusion.15
  714.8 1072.3 %all-reduce.3.cloned.1.call-done = f32[128,1024]{1,0:T(8,128)} async-done(((f32[128,1024]{1,0:T(8,128)}), f32[128,1024]{1,0:T(8,128)}) %all-reduce.3.cloned.1.call-update) | async-done | bytes 524304 | tf_op jit(solution)/shard_map/psum | solution.py:70
  1787.0 1.9 copy.85
  (13 shorter events, 0.2 us)
Async XLA Ops:
  7.2 4.8 copy-start.5
  7.2 4.8 copy-start.2
  7.2 1779.8 %all-reduce.3.cloned.1.call-start = ((), (), s32[]{:S(2)}) async-start(), calls=%async_computation | async-start | bytes 1048576 | tf_op jit(solution)/shard_map/psum | solution.py:70
  8.4 10.3 copy-start.8
  8.4 10.6 copy-start.6
  8.4 13.2 collective-permute-start
  12.1 6.9 copy-start.9
  12.1 39.1 %collective-permute-start.1 = (bf16[127,1024]{1,0:T(8,128)(2,1)S(1)}, bf16[127,1024]{1,0:T(8,128)(2,1)S(1)}, u32[]{:S(2)}, u32[]{:S(2)}) collective-permute-start(bf16[127,1024]{1,0:T(8,128)(2,1)S(1)} %bitcast.62), channel_id=1, source_target_pairs={{8,0},{16,8},{24,16},{32,24},{40,32},{48,40},{56,48},{64,56},{72,6... | collective-permute-start | bytes 780296 | tf_op jit(solution)/shard_map/ppermute | solution.py:12
  22.0 0.7 copy-start.10
  23.4 1.0 copy-start.3
  51.2 7.4 copy-start.4
  76.2 616.3 %collective-permute-start.2 = (bf16[6,1024]{1,0:T(8,128)(2,1)S(1)}, bf16[6,1024]{1,0:T(8,128)(2,1)S(1)}, u32[]{:S(2)}, u32[]{:S(2)}) collective-permute-start(bf16[6,1024]{1,0:T(8,128)(2,1)S(1)} %slice.24), channel_id=1, source_target_pairs={{8,0},{16,8},{24,16},{32,24},{40,32},{48,40},{56,48},{64,56},{72,6... | collective-permute-start | bytes 36872 | tf_op jit(solution)/shard_map/ppermute | solution.py:12
  79.6 615.9 %collective-permute-start.3 = (bf16[127,1024]{1,0:T(8,128)(2,1)S(1)}, bf16[127,1024]{1,0:T(8,128)(2,1)S(1)}, u32[]{:S(2)}, u32[]{:S(2)}) collective-permute-start(bf16[127,1024]{1,0:T(8,128)(2,1)S(1)} %slice.27), channel_id=1, source_target_pairs={{0,8},{8,16},{16,24},{24,32},{32,40},{40,48},{48,56},{56,64},{64,7... | collective-permute-start | bytes 780296 | tf_op jit(solution)/shard_map/ppermute | solution.py:12
  693.5 1.0 copy-start
  693.5 1.0 copy-start.1
  705.6 0.9 copy-start.7
Sparse Core Ops, SparseCore 0:
  705.8 1081.1 all-reduce.2
where the time goes:
time: 1800 us
  waiting for transfers between devices  1070 us (59%)
  blocking collectives  651 us (36%)
  matrix products  23.8 us (1%)
    psum x1, waiting for transfers between devices, shards(): grad_filter_mr = lax.psum(local_filter_mr, 'ctx')  1070 us
    psum x1, blocking collectives, shards(): grad_filter_se, grad_gain = lax.psum((local_filter_se, local_gain), 'ctx')  610 us
    psum x2, blocking collectives, token_total(): return lax.psum(partial_sum, 'tp')  40.9 us
  transfers between devices with their start and end apart: 5, of which 1 were waited for; matrix products, arithmetic and copies ran while one was open for 1% of the time, Pallas kernels for 0%

commit v1 on v0

v1 whole, which is shorter than its diff:
```python
import jax
import jax.numpy as jnp
from jax import lax
from jax.sharding import PartitionSpec as P

D = 8192


def shifted(block, axis, distance):
    devices = range(lax.axis_size(axis))
    route = [(i - distance, i) for i in devices if i - distance in devices]
    return lax.ppermute(block, axis, route)


def depthwise(lhs, kernel):
    out = lax.conv_general_dilated(
        lhs[None],
        kernel[:, None, :],
        (1,),
        "VALID",
        dimension_numbers=("NWC", "WIO", "NWC"),
        feature_group_count=lhs.shape[1],
        preferred_element_type=jnp.float32,
    )
    return out[0]


def from_left(block, width):
    return shifted(block[block.shape[0] - width :], "ctx", 1)


def from_right(block, width):
    return shifted(block[:width], "ctx", -1)


def token_totals(parts):
    n = lax.axis_size("tp")
    spread = jnp.broadcast_to(parts[None], (n,) + parts.shape)
    return jnp.sum(lax.all_to_all(spread, "tp", 0, 0, tiled=True), axis=0)


def filter_totals(mr, small):
    bf16 = jnp.bfloat16
    n = lax.axis_size("ctx")
    taps, cols = mr.shape
    blocks = cols // 128
    groups = taps // 8
    tiles = mr.reshape(groups, 8, blocks, 128).transpose(0, 2, 1, 3).reshape(n, 8, 128)
    rows = small.reshape(8 * blocks, 1, 128)
    rows = jnp.pad(rows, ((0, n - 8 * blocks), (0, 0), (0, 0)))
    packed = jnp.concatenate([tiles, rows], axis=1).astype(bf16)
    packed = jnp.pad(packed, ((0, 0), (0, 7), (0, 0)))
    got = lax.all_to_all(packed, "ctx", 0, 0, tiled=True)
    total = lax.optimization_barrier(jnp.sum(got.astype(jnp.float32), axis=0)).astype(bf16)
    spread = jnp.broadcast_to(total[None], (n,) + total.shape)
    back = lax.all_to_all(spread, "ctx", 0, 0, tiled=True).astype(jnp.float32)
    mr_sum = back[:, :8].reshape(groups, blocks, 8, 128).transpose(0, 2, 1, 3).reshape(taps, cols)
    small_sum = back[: 8 * blocks, 8].reshape(8, cols)
    return mr_sum, small_sum


def shards(
    value_path, key_se, query_se, key_mr, query_mr, out_grad, norm_gain, filter_se, filter_mr
):
    f32 = jnp.float32
    bf16 = jnp.bfloat16
    se_taps = filter_se.shape[0]
    mr_taps = filter_mr.shape[0]
    prod_se = (key_se.astype(f32) * value_path.astype(f32)).astype(bf16)
    grad_conv_mr = (out_grad.astype(f32) * query_mr.astype(f32)).astype(bf16)
    rim_se = from_left(prod_se, se_taps - 1)
    rim_grad_mr = from_right(grad_conv_mr, mr_taps - 1)
    pad_se = jnp.concatenate([rim_se, prod_se], axis=0)
    pad_grad_mr = jnp.concatenate([grad_conv_mr, rim_grad_mr], axis=0)
    conv_se = depthwise(pad_se, filter_se[::-1])
    mixed_se = query_se.astype(f32) * conv_se
    grad_prod_mr = depthwise(pad_grad_mr, filter_mr)
    gain = norm_gain.astype(f32)
    grad_normed = grad_prod_mr * key_mr.astype(f32)
    scaled = grad_normed * gain
    square_part = jnp.sum(mixed_se * mixed_se, axis=1)
    dot_part = jnp.sum(scaled * mixed_se, axis=1)
    totals = token_totals(jnp.stack([square_part, dot_part]))
    inv_rms = lax.rsqrt(totals[0][:, None] / D + 1e-06)
    dot_sum = totals[1][:, None]
    normed = (mixed_se * inv_rms * gain).astype(bf16)
    prod_mr = (key_mr.astype(f32) * normed.astype(f32)).astype(bf16)
    grad_mixed = inv_rms * scaled - mixed_se * (inv_rms * inv_rms * inv_rms) * dot_sum / D
    grad_conv_se = (grad_mixed * query_se.astype(f32)).astype(bf16)
    rim_mr = from_left(prod_mr, mr_taps - 1)
    rim_grad_se = from_right(grad_conv_se, se_taps - 1)
    grad_key_mr = (grad_prod_mr * normed.astype(f32)).astype(bf16)
    grad_query_se = (grad_mixed * conv_se).astype(bf16)
    local_filter_mr = depthwise(pad_grad_mr, prod_mr)
    local_gain = jnp.sum(grad_normed * mixed_se * inv_rms, axis=0)
    local_filter_se = depthwise(pad_se, grad_conv_se)[::-1]
    grad_filter_mr, small = filter_totals(
        local_filter_mr, jnp.concatenate([local_filter_se, local_gain[None]], axis=0)
    )
    pad_mr = jnp.concatenate([rim_mr, prod_mr], axis=0)
    conv_mr = depthwise(pad_mr, filter_mr[::-1])
    grad_query_mr = (out_grad.astype(f32) * conv_mr).astype(bf16)
    grad_prod_se = depthwise(jnp.concatenate([grad_conv_se, rim_grad_se], axis=0), filter_se)
    grad_key_se = (grad_prod_se * value_path.astype(f32)).astype(bf16)
    grad_value = (grad_prod_se * key_se.astype(f32)).astype(bf16)
    return (
        grad_value,
        grad_query_se,
        grad_key_se,
        grad_query_mr,
        grad_key_mr,
        small[:se_taps],
        grad_filter_mr,
        small[se_taps],
    )


def solution(mesh):
    wide = P("ctx", "tp")
    return jax.shard_map(
        shards,
        mesh=mesh,
        in_specs=(wide,) * 6 + (P("tp"), P(None, "tp"), P(None, "tp")),
        out_specs=(wide,) * 5 + (P(None, "tp"), P(None, "tp"), P("tp")),
        check_vma=False,
    )
```

time: 1800 us -> 134 us (0.07)
  the two profiles are of different devices: /device:TPU:128 before, /device:TPU:2 now
where the time goes in v1:
time: 134 us; the launch traced here: 133 us
  starting transfers between devices  50.3 us (38%)
  matrix products  25.4 us (19%)
  waiting for transfers between devices  25.2 us (19%)
  blocking collectives  16.1 us (12%)
  local copies, waits for them, and re-layouts  8.77 us (7%)
  other arithmetic  6.01 us (4%)
    conv_general_dilated x6, matrix products, depthwise(): lax.conv_general_dilated(lhs[None], kernel[:, None, :], (1,), 'VALID', di...  25.4 us
    ppermute x4, starting transfers between devices, shifted(): return lax.ppermute(block, axis, route)  22.2 us
    all_to_all x1, starting transfers between devices, filter_totals(): got = lax.all_to_all(packed, 'ctx', 0, 0, tiled=True)  16.6 us
    all_to_all x1, blocking collectives, token_totals(): return jnp.sum(lax.all_to_all(spread, 'tp', 0, 0, tiled=True), axis=0)  16.1 us
    all_to_all x1, waiting for transfers between devices, filter_totals(): back = lax.all_to_all(spread, 'ctx', 0, 0, tiled=True).astype(jnp.float32)  12.6 us
    all_to_all x1, starting transfers between devices, filter_totals(): back = lax.all_to_all(spread, 'ctx', 0, 0, tiled=True).astype(jnp.float32)  11.5 us
    ppermute x4, waiting for transfers between devices, shifted(): return lax.ppermute(block, axis, route)  9.87 us
    all_to_all x1, waiting for transfers between devices, filter_totals(): got = lax.all_to_all(packed, 'ctx', 0, 0, tiled=True)  2.82 us
  transfers between devices with their start and end apart: 6, of which 5 were waited for; matrix products, arithmetic and copies ran while one was open for 10% of the time, Pallas kernels for 0%

profile of v1, /device:TPU:2, one launch (start us, length us, event | category | flops | bytes accessed | tf_op | source)
XLA Modules:
  0.0 133.0 jit_solution(13575091597516982039)
XLA Ops:
  0.6 0.0 copy-start.7
  0.6 0.0 copy-start.2
  0.7 1.2 fusion.13
  1.8 0.0 copy-start.10
  1.8 3.4 %collective-permute-start = (bf16[6,1024]{1,0:T(8,128)(2,1)S(1)}, bf16[6,1024]{1,0:T(8,128)(2,1)S(1)}, u32[]{:S(2)}, u32[]{:S(2)}) collective-permute-start(bf16[6,1024]{1,0:T(8,128)(2,1)S(1)} %slice.48), channel_id=1, source_target_pairs={{0,8},{8,16},{16,24},{24,32},{32,40},{40,48},{48,56},{56,64},{64,7... | collective-permute-start | bytes 36872 | tf_op jit(solution)/shard_map/ppermute | solution.py:12
  5.3 0.1 fusion.15
  5.3 0.0 copy-start.11
  5.4 13.0 %collective-permute-start.1 = (bf16[127,1024]{1,0:T(8,128)(2,1)S(1)}, bf16[127,1024]{1,0:T(8,128)(2,1)S(1)}, u32[]{:S(2)}, u32[]{:S(2)}) collective-permute-start(bf16[127,1024]{1,0:T(8,128)(2,1)S(1)} %bitcast.77), channel_id=1, source_target_pairs={{8,0},{16,8},{24,16},{32,24},{40,32},{48,40},{56,48},{64,56},{72,6... | collective-permute-start | bytes 780296 | tf_op jit(solution)/shard_map/ppermute | solution.py:12
  18.3 0.0 copy-done.10
  18.4 0.2 rev.9
  18.6 0.0 collective-permute-done
  18.6 0.1 maximum_bitcast_fusion.2
  18.7 0.1 reshape.66
  18.9 0.2 copy.84
  19.0 0.0 copy-start.12
  19.1 0.6 copy-done.12
  19.7 0.3 convolution_select_fusion.1
  20.0 0.3 copy.86
  20.4 0.1 reshape.70
  20.5 0.0 copy-start.8
  20.5 1.7 %collective-permute-done.1 = bf16[127,1024]{1,0:T(8,128)(2,1)S(1)} collective-permute-done((bf16[127,1024]{1,0:T(8,128)(2,1)S(1)}, bf16[127,1024]{1,0:T(8,128)(2,1)S(1)}, u32[]{:S(2)}, u32[]{:S(2)}) %collective-permute-start.1) | collective-permute-done | bytes 260128 | tf_op jit(solution)/shard_map/ppermute | solution.py:12
  22.3 0.0 copy-start.5
  22.3 0.8 copy-done.5
  23.1 0.0 copy-done.8
  23.1 7.3 %fusion.5 = f32[1,128,1024]{2,0,1:T(1,128)S(1)} fusion(bf16[1,255,1024]{2,1,0:T(8,128)(2,1)S(1)} %maximum_bitcast_fusion, bf16[128,1,1024]{2,0,1:T(8,128)(2,1)S(1)} %bitcast.80), kind=kOutput, calls=%fused_computation.10 | convolution fusion | flops 33554432 | bytes 1308672 | tf_op jit(solution)/shard_map/conv_general_dilated | solution.py:16
  30.4 0.3 multiply_reduce_fusion.2
  30.7 16.1 %all_to_all.15 = f32[8,2,128]{2,1,0:T(2,128)S(1)} all-to-all(f32[8,2,128]{2,1,0:T(2,128)S(1)} %broadcast_in_dim.54), channel_id=1, replica_groups=mesh['ctx'=128,'tp'=8] {'tp'}, dimensions={0} | all-to-all | bytes 16384 | tf_op jit(solution)/shard_map/all_to_all | solution.py:39
  46.8 1.3 multiply_convert_fusion.1
  48.1 1.1 fusion.9
  49.3 0.2 rev.11
  49.6 9.0 %fusion = bf16[128,1024]{1,0:T(8,128)(2,1)S(1)} fusion(bf16[1,255,1024]{2,1,0:T(8,128)(2,1)S(1)} %copy-done.6, bf16[128,1,1024]{2,0,1:T(8,128)(2,1)S(1)} %bitcast.74), kind=kOutput, calls=%fused_computation.3 | convolution fusion | flops 33685504 | bytes 1046528 | tf_op jit(solution)/shard_map/conv_general_dilated | solution.py:16
  58.7 0.1 fusion.19
  58.8 0.9 pad.10
  59.7 16.6 %all-to-all-start.1 = ((bf16[128,16,128]{2,1,0:T(8,128)(2,1)}), bf16[128,16,128]{2,1,0:T(8,128)(2,1)S(1)}, u32[]{:S(2)}, u32[]{:S(2)}) async-start(bf16[128,16,128]{2,1,0:T(8,128)(2,1)} %pad.10), calls=%async_computation.1 | async-start | bytes 1048576 | tf_op jit(solution)/shard_map/all_to_all | solution.py:53
  76.3 2.8 %collective-permute-start.2 = (bf16[6,1024]{1,0:T(8,128)(2,1)S(1)}, bf16[6,1024]{1,0:T(8,128)(2,1)S(1)}, u32[]{:S(2)}, u32[]{:S(2)}) collective-permute-start(bf16[6,1024]{1,0:T(8,128)(2,1)S(1)} %slice.52), channel_id=1, source_target_pairs={{8,0},{16,8},{24,16},{32,24},{40,32},{48,40},{56,48},{64,56},{72,6... | collective-permute-start | bytes 36872 | tf_op jit(solution)/shard_map/ppermute | solution.py:12
  79.1 0.0 copy-done.9
  79.1 0.3 rev.10
  79.4 0.1 slice.55
  79.5 3.0 %collective-permute-start.3 = (bf16[127,1024]{1,0:T(8,128)(2,1)S(1)}, bf16[127,1024]{1,0:T(8,128)(2,1)}, u32[]{:S(2)}, u32[]{:S(2)}) collective-permute-start(bf16[127,1024]{1,0:T(8,128)(2,1)S(1)} %slice.55), channel_id=1, source_target_pairs={{0,8},{8,16},{16,24},{24,32},{32,40},{40,48},{48,56},{56,64},{64,7... | collective-permute-start | bytes 780296 | tf_op jit(solution)/shard_map/ppermute | solution.py:12
  82.5 5.2 %collective-permute-done.2 = bf16[6,1024]{1,0:T(8,128)(2,1)S(1)} collective-permute-done((bf16[6,1024]{1,0:T(8,128)(2,1)S(1)}, bf16[6,1024]{1,0:T(8,128)(2,1)S(1)}, u32[]{:S(2)}, u32[]{:S(2)}) %collective-permute-start.2) | collective-permute-done | bytes 12320 | tf_op jit(solution)/shard_map/ppermute | solution.py:12
  87.8 0.1 reshape.73
  87.9 0.2 copy.91
  88.1 0.3 convolution_select_fusion
  88.5 0.3 copy.93
  88.8 0.0 copy-start
  88.8 0.0 copy-start.1
  88.8 0.1 reshape.77
  88.9 0.8 copy-done
  89.8 0.1 copy-done.1
  89.9 0.9 fusion.14
  90.8 2.9 %collective-permute-done.3 = bf16[127,1024]{1,0:T(8,128)(2,1)} collective-permute-done((bf16[127,1024]{1,0:T(8,128)(2,1)S(1)}, bf16[127,1024]{1,0:T(8,128)(2,1)}, u32[]{:S(2)}, u32[]{:S(2)}) %collective-permute-start.3) | collective-permute-done | bytes 260128 | tf_op jit(solution)/shard_map/ppermute | solution.py:12
  93.7 1.0 maximum_bitcast_fusion.1
  94.7 2.8 %all-to-all-done.1 = bf16[128,16,128]{2,1,0:T(8,128)(2,1)S(1)} async-done(((bf16[128,16,128]{2,1,0:T(8,128)(2,1)}), bf16[128,16,128]{2,1,0:T(8,128)(2,1)S(1)}, u32[]{:S(2)}, u32[]{:S(2)}) %all-to-all-start.1) | async-done | bytes 524320 | tf_op jit(solution)/shard_map/all_to_all | solution.py:53
  97.6 0.1 convert_reduce_fusion
  97.7 0.9 broadcast_in_dim.62
  98.6 11.5 %all-to-all-start.2 = ((bf16[128,16,128]{2,1,0:T(8,128)(2,1)}), bf16[128,16,128]{2,1,0:T(8,128)(2,1)S(1)}, u32[]{:S(2)}, u32[]{:S(2)}) async-start(bf16[128,16,128]{2,1,0:T(8,128)(2,1)} %broadcast_in_dim.62), calls=%async_computation.2 | async-start | bytes 1048576 | tf_op jit(solution)/shard_map/all_to_all | solution.py:56
  110.1 7.3 %fusion.2 = f32[1,128,1024]{2,0,1:T(1,128)S(1)} fusion(bf16[1,255,1024]{2,1,0:T(8,128)(2,1)S(1)} %maximum_bitcast_fusion.1, bf16[128,1,1024]{2,0,1:T(8,128)(2,1)S(1)} %bitcast.81), kind=kOutput, calls=%fused_computation.7 | convolution fusion | flops 33554432 | bytes 1308672 | tf_op jit(solution)/shard_map/conv_general_dilated | solution.py:16
  117.4 0.8 fusion.16
  118.3 12.6 %all-to-all-done.2 = bf16[128,16,128]{2,1,0:T(8,128)(2,1)S(1)} async-done(((bf16[128,16,128]{2,1,0:T(8,128)(2,1)}), bf16[128,16,128]{2,1,0:T(8,128)(2,1)S(1)}, u32[]{:S(2)}, u32[]{:S(2)}) %all-to-all-start.2) | async-done | bytes 524320 | tf_op jit(solution)/shard_map/all_to_all | solution.py:56
  130.8 0.1 convert_element_type.94
  130.9 0.1 slice_reduce_fusion
  131.0 0.6 slice.41
  131.6 0.8 slice.57
  132.4 0.6 slice.58
  (30 shorter events, 0.4 us)
Async XLA Ops:
  0.6 4.6 %copy-start.7 = (bf16[128,1024]{1,0:T(8,128)(2,1)S(1)}, bf16[128,1024]{1,0:T(8,128)(2,1)}, u32[]{:S(2)}) copy-start(bf16[128,1024]{1,0:T(8,128)(2,1)} %param.13) | copy-start | bytes 786436
  0.6 4.6 %copy-start.2 = (bf16[128,1024]{1,0:T(8,128)(2,1)S(1)}, bf16[128,1024]{1,0:T(8,128)(2,1)}, u32[]{:S(2)}) copy-start(bf16[128,1024]{1,0:T(8,128)(2,1)} %param.14) | copy-start | bytes 786436
  1.8 16.5 %copy-start.10 = (bf16[7,1024]{1,0:T(8,128)(2,1)S(1)}, bf16[7,1024]{1,0:T(8,128)(2,1)}, u32[]{:S(2)}) copy-start(bf16[7,1024]{1,0:T(8,128)(2,1)} %param.16) | copy-start | bytes 43012
  1.8 16.8 %collective-permute-start = (bf16[6,1024]{1,0:T(8,128)(2,1)S(1)}, bf16[6,1024]{1,0:T(8,128)(2,1)S(1)}, u32[]{:S(2)}, u32[]{:S(2)}) collective-permute-start(bf16[6,1024]{1,0:T(8,128)(2,1)S(1)} %slice.48), channel_id=1, source_target_pairs={{0,8},{8,16},{16,24},{24,32},{32,40},{40,48},{48,56},{56,64},{64,7... | collective-permute-start | bytes 36872 | tf_op jit(solution)/shard_map/ppermute | solution.py:12
  5.3 13.3 %copy-start.11 = (bf16[1024]{0:T(1024)(128)(2,1)S(1)}, bf16[1024]{0:T(1024)(128)(2,1)}, u32[]{:S(2)}) copy-start(bf16[1024]{0:T(1024)(128)(2,1)} %param.15) | copy-start | bytes 6148
  5.4 16.9 %collective-permute-start.1 = (bf16[127,1024]{1,0:T(8,128)(2,1)S(1)}, bf16[127,1024]{1,0:T(8,128)(2,1)S(1)}, u32[]{:S(2)}, u32[]{:S(2)}) collective-permute-start(bf16[127,1024]{1,0:T(8,128)(2,1)S(1)} %bitcast.77), channel_id=1, source_target_pairs={{8,0},{16,8},{24,16},{32,24},{40,32},{48,40},{56,48},{64,56},{72,6... | collective-permute-start | bytes 780296 | tf_op jit(solution)/shard_map/ppermute | solution.py:12
  19.0 0.7 copy-start.12
  20.5 2.6 %copy-start.8 = (bf16[128,1024]{1,0:T(8,128)(2,1)S(1)}, bf16[128,1024]{1,0:T(8,128)(2,1)}, u32[]{:S(2)}) copy-start(bf16[128,1024]{1,0:T(8,128)(2,1)} %param.17) | copy-start | bytes 786436
  22.3 0.8 copy-start.5
  23.1 7.3 %copy-start.3 = (bf16[128,1024]{1,0:T(8,128)(2,1)S(1)}, bf16[128,1024]{1,0:T(8,128)(2,1)}, u32[]{:S(2)}) copy-start(bf16[128,1024]{1,0:T(8,128)(2,1)} %param.12) | copy-start | bytes 786436
  23.1 7.3 %copy-start.4 = (bf16[128,1024]{1,0:T(8,128)(2,1)S(1)}, bf16[128,1024]{1,0:T(8,128)(2,1)}, u32[]{:S(2)}) copy-start(bf16[128,1024]{1,0:T(8,128)(2,1)} %param.11) | copy-start | bytes 786436
  48.1 1.5 %copy-start.6 = (bf16[1,255,1024]{2,1,0:T(8,128)(2,1)S(1)}, bf16[1,255,1024]{2,1,0:T(8,128)(2,1)}, u32[]{:S(2)}) copy-start(bf16[1,255,1024]{2,1,0:T(8,128)(2,1)} %copy-done.5) | copy-start | bytes 1566724
  59.7 19.4 %copy-start.9 = (bf16[128,1024]{1,0:T(8,128)(2,1)S(1)}, bf16[128,1024]{1,0:T(8,128)(2,1)}, u32[]{:S(2)}) copy-start(bf16[128,1024]{1,0:T(8,128)(2,1)} %param.17) | copy-start | bytes 786436
  59.7 37.9 %all-to-all-start.1 = ((bf16[128,16,128]{2,1,0:T(8,128)(2,1)}), bf16[128,16,128]{2,1,0:T(8,128)(2,1)S(1)}, u32[]{:S(2)}, u32[]{:S(2)}) async-start(bf16[128,16,128]{2,1,0:T(8,128)(2,1)} %pad.10), calls=%async_computation.1 | async-start | bytes 1048576 | tf_op jit(solution)/shard_map/all_to_all | solution.py:53
  76.3 11.5 %collective-permute-start.2 = (bf16[6,1024]{1,0:T(8,128)(2,1)S(1)}, bf16[6,1024]{1,0:T(8,128)(2,1)S(1)}, u32[]{:S(2)}, u32[]{:S(2)}) collective-permute-start(bf16[6,1024]{1,0:T(8,128)(2,1)S(1)} %slice.52), channel_id=1, source_target_pairs={{8,0},{16,8},{24,16},{32,24},{40,32},{48,40},{56,48},{64,56},{72,6... | collective-permute-start | bytes 36872 | tf_op jit(solution)/shard_map/ppermute | solution.py:12
  79.5 14.2 %collective-permute-start.3 = (bf16[127,1024]{1,0:T(8,128)(2,1)S(1)}, bf16[127,1024]{1,0:T(8,128)(2,1)}, u32[]{:S(2)}, u32[]{:S(2)}) collective-permute-start(bf16[127,1024]{1,0:T(8,128)(2,1)S(1)} %slice.55), channel_id=1, source_target_pairs={{0,8},{8,16},{16,24},{24,32},{32,40},{40,48},{48,56},{56,64},{64,7... | collective-permute-start | bytes 780296 | tf_op jit(solution)/shard_map/ppermute | solution.py:12
  88.8 1.0 copy-start
  88.8 1.0 copy-start.1
  98.6 32.3 %all-to-all-start.2 = ((bf16[128,16,128]{2,1,0:T(8,128)(2,1)}), bf16[128,16,128]{2,1,0:T(8,128)(2,1)S(1)}, u32[]{:S(2)}, u32[]{:S(2)}) async-start(bf16[128,16,128]{2,1,0:T(8,128)(2,1)} %broadcast_in_dim.62), calls=%async_computation.2 | async-start | bytes 1048576 | tf_op jit(solution)/shard_map/all_to_all | solution.py:56

commit v2 on v1

v2 whole, which is shorter than its diff:
```python
import jax
import jax.numpy as jnp
import numpy as np
from jax import lax
from jax.experimental import pallas as pl
from jax.experimental.pallas import tpu as pltpu
from jax.sharding import PartitionSpec as P

D = 8192
WIDTH = 256
HALO = 16
F32 = jnp.float32
BF16 = jnp.bfloat16


def split(matrix):
    high = matrix.astype(jnp.bfloat16)
    low = (matrix - high.astype(np.float64)).astype(jnp.bfloat16)
    return high, low


def transforms():
    phase = 2 * np.pi * np.outer(np.arange(128) + 0.5, np.arange(256)) / 256
    forward = np.concatenate([np.cos(phase), -np.sin(phase)], axis=0)
    inverse = forward.T / 128
    f_high, f_low = split(forward)
    i_high, i_low = split(inverse)
    whole = np.concatenate([f_high, f_low], axis=1)
    half = np.concatenate([f_high[:, :128], f_low[:, :128]], axis=1)
    back = np.concatenate([i_high, i_high, i_low], axis=1)
    return jnp.asarray(whole), jnp.asarray(half), jnp.asarray(back[:128]), jnp.asarray(back[128:])


def to_spectrum(matrix, *rows):
    return jnp.dot(matrix, jnp.concatenate(rows + rows, axis=0), preferred_element_type=F32)


def from_spectrum(matrix, re, im):
    both = jnp.concatenate([re, im], axis=0)
    high = both.astype(BF16)
    low = (both - high.astype(F32)).astype(BF16)
    return jnp.dot(matrix, jnp.concatenate([high, low, high], axis=0), preferred_element_type=F32)


def correlated(matrix, kernel, signal):
    k_re, k_im = kernel[:128], kernel[128:]
    s_re, s_im = signal[:128], signal[128:]
    return from_spectrum(matrix, k_re * s_re + k_im * s_im, k_re * s_im - k_im * s_re)


def convolved(matrix, kernel, signal):
    k_re, k_im = kernel[:128], kernel[128:]
    s_re, s_im = signal[:128], signal[128:]
    return from_spectrum(matrix, k_re * s_re - k_im * s_im, k_re * s_im + k_im * s_re)


def lane_blocks(value):
    return sum(value[:, i : i + 128] for i in range(0, value.shape[1], 128))


def se_window(win, rim, key, value):
    prod = (key[...].astype(F32) * value[...].astype(F32)).astype(BF16)
    win[0:HALO] = rim[...].astype(F32)
    win[HALO:] = prod.astype(F32)


def se_kernel(key, value, query, rim, taps, conv, mixed, square, win):
    se_window(win, rim, key, value)
    f = taps[...].astype(F32)
    total = f[0:1] * win[HALO : HALO + 128]
    for j in range(1, f.shape[0]):
        total = total + f[j : j + 1] * win[HALO - j : HALO - j + 128]
    conv[...] = total
    m = query[...].astype(F32) * total
    mixed[...] = m

    @pl.when(pl.program_id(0) == 0)
    def _():
        square[...] = jnp.zeros_like(square)

    square[...] += lane_blocks(m * m)


def dot_kernel(
    grad, rim, taps, key, gain, mixed, square, whole, half, back, prod, spectrum, stats, acc
):
    kernel = to_spectrum(half[...], taps[...])
    signal = to_spectrum(whole[...], grad[...], rim[...])
    spectrum[...] = signal
    gp = correlated(back[...], kernel, signal)
    prod[...] = gp
    scaled = gp * key[...].astype(F32) * gain[...].astype(F32)

    @pl.when(pl.program_id(0) == 0)
    def _():
        acc[...] = jnp.zeros_like(acc)

    acc[...] += lane_blocks(scaled * mixed[...])

    @pl.when(pl.program_id(0) == pl.num_programs(0) - 1)
    def _():
        squares = jnp.sum(square[...].T, axis=0, keepdims=True)
        dots = jnp.sum(acc[...].T, axis=0, keepdims=True)
        row = lax.broadcasted_iota(jnp.int32, (8, 128), 0)
        both = jnp.where(row == 0, squares, jnp.where(row == 1, dots, 0.0))
        stats[...] = jnp.broadcast_to(both[None], stats.shape)


def main_kernel(
    stats, mixed, conv, prod, spectrum, key_mr, query_se, key_se, value, rim, gain, half, back,
    out_query_se, out_key_mr, out_prod_mr, out_conv_se, out_head, out_filter, out_small,
    win, inv_cols, dot_cols,
):
    @pl.when(pl.program_id(0) == 0)
    def _():
        sums = jnp.sum(stats[...], axis=0)
        inv = lax.rsqrt(sums[0:1] / D + 1e-06)
        dot = inv * inv * inv * sums[1:2] / D
        inv_cols[...] = jnp.broadcast_to(inv, (128, 128)).T
        dot_cols[...] = jnp.broadcast_to(dot, (128, 128)).T

    reps = mixed.shape[1] // 128
    inv = jnp.concatenate([inv_cols[...]] * reps, axis=1)
    dot = jnp.concatenate([dot_cols[...]] * reps, axis=1)
    m = mixed[...]
    gp = prod[...]
    g = gain[...].astype(F32)
    k = key_mr[...].astype(F32)
    scaled_mixed = m * inv
    normed = (scaled_mixed * g).astype(BF16).astype(F32)
    p = (k * normed).astype(BF16)
    out_prod_mr[...] = p
    out_key_mr[...] = (gp * normed).astype(BF16)
    grad = correlated(back[...], to_spectrum(half[...], p), spectrum[...])
    for b in range(reps):
        tile = grad[:, 128 * b : 128 * b + 128].reshape(out_filter.shape[0], 8, 128)
        out_filter[:, b] = tile.astype(BF16)
    grad_normed = gp * k
    gain_row = jnp.sum(grad_normed * scaled_mixed, axis=0, keepdims=True)
    grad_mixed = inv * (grad_normed * g) - m * dot
    out_query_se[...] = (grad_mixed * conv[...]).astype(BF16)
    gcs = (grad_mixed * query_se[...].astype(F32)).astype(BF16)
    out_conv_se[...] = gcs
    out_head[...] = gcs[:HALO]
    gcs = gcs.astype(F32)
    se_window(win, rim, key_se, value)
    taps = out_small.shape[0] - 1
    rows = [
        jnp.sum(gcs * win[HALO - j : HALO - j + 128], axis=0, keepdims=True) for j in range(taps)
    ]
    out_small[...] = jnp.concatenate(rows + [gain_row], axis=0)


def last_kernel(
    prod_mr, rim_mr, out_grad, taps_mr, conv_se, rim_se, taps_se, value, key_se, whole, half, back,
    out_query_mr, out_key_se, out_value, win,
):
    kernel = to_spectrum(half[...], taps_mr[...])
    signal = to_spectrum(whole[...], rim_mr[...], prod_mr[...])
    conv = convolved(back[...], kernel, signal)
    out_query_mr[...] = (out_grad[...].astype(F32) * conv).astype(BF16)
    win[0:128] = conv_se[...].astype(F32)
    win[128:] = rim_se[...].astype(F32)
    f = taps_se[...].astype(F32)
    total = f[0:1] * win[0:128]
    for j in range(1, f.shape[0]):
        total = total + f[j : j + 1] * win[j : j + 128]
    out_key_se[...] = (total * value[...].astype(F32)).astype(BF16)
    out_value[...] = (total * key_se[...].astype(F32)).astype(BF16)


def wide(rows):
    return pl.BlockSpec((rows, WIDTH), lambda i: (0, i))


def fixed(*shape):
    return pl.BlockSpec(shape, lambda i: (0,) * len(shape))


def call(kernel, cols, in_specs, out_specs, out_shape, scratch, flops, moved):
    return pl.pallas_call(
        kernel,
        grid=(cols // WIDTH,),
        in_specs=in_specs,
        out_specs=out_specs,
        out_shape=[jax.ShapeDtypeStruct(s, d) for s, d in out_shape],
        scratch_shapes=scratch,
        compiler_params=pltpu.CompilerParams(vmem_limit_bytes=40 * 1024 * 1024),
        cost_estimate=pl.CostEstimate(flops=flops, bytes_accessed=moved, transcendentals=0),
    )


def shifted(block, axis, distance):
    devices = range(lax.axis_size(axis))
    route = [(i - distance, i) for i in devices if i - distance in devices]
    return lax.ppermute(block, axis, route)


def filter_totals(tiles, small):
    n = lax.axis_size("ctx")
    cols = small.shape[1]
    rows = small.reshape(-1, 1, 1, 128).astype(BF16)
    rows = jnp.pad(rows, ((0, n - rows.shape[0]), (0, 0), (0, 1), (0, 0)))
    packed = jnp.concatenate([tiles.reshape(n, 4, 2, 128), rows], axis=1)
    got = lax.all_to_all(packed, "ctx", 0, 0, tiled=True)
    total = lax.optimization_barrier(jnp.sum(got.astype(F32), axis=0)).astype(BF16)
    spread = jnp.broadcast_to(total[None], (n,) + total.shape)
    back = lax.all_to_all(spread, "ctx", 0, 0, tiled=True)
    mr_sum = back[:, :4].reshape(tiles.shape).astype(F32).transpose(0, 2, 1, 3).reshape(-1, cols)
    small_sum = back[: cols // 16, 4, 0].astype(F32).reshape(8, cols)
    return mr_sum, small_sum


def shards(
    value_path, key_se, query_se, key_mr, query_mr, out_grad, norm_gain, filter_se, filter_mr
):
    tokens, cols = value_path.shape
    se_taps = filter_se.shape[0]
    full = (tokens, cols)
    whole, half, back_first, back_last = transforms()
    gain = norm_gain.reshape(1, cols)
    tail = (key_se[-HALO:].astype(F32) * value_path[-HALO:].astype(F32)).astype(BF16)
    grad_conv_mr = (out_grad.astype(F32) * query_mr.astype(F32)).astype(BF16)
    rim_se = shifted(tail, "ctx", 1)
    rim_grad_mr = shifted(grad_conv_mr, "ctx", -1)
    mats = [fixed(*whole.shape), fixed(*half.shape), fixed(*back_first.shape)]
    conv_se, mixed_se, square = call(
        se_kernel,
        cols,
        [wide(tokens)] * 3 + [wide(HALO), wide(se_taps)],
        [wide(tokens), wide(tokens), fixed(tokens, 128)],
        [(full, F32), (full, F32), ((tokens, 128), F32)],
        [pltpu.VMEM((tokens + HALO, WIDTH), F32)],
        18 * tokens * cols,
        14 * tokens * cols,
    )(key_se, value_path, query_se, rim_se, filter_se)
    grad_prod_mr, spectrum, stats = call(
        dot_kernel,
        cols,
        [wide(tokens)] * 4 + [wide(1), wide(tokens), fixed(tokens, 128)] + mats,
        [wide(tokens), wide(2 * tokens), fixed(8, 8, 128)],
        [(full, F32), ((2 * tokens, cols), F32), ((8, 8, 128), F32)],
        [pltpu.VMEM((tokens, 128), F32)],
        3000 * tokens * cols,
        24 * tokens * cols,
    )(grad_conv_mr, rim_grad_mr, filter_mr, key_mr, gain, mixed_se, square, whole, half, back_first)
    stats = lax.all_to_all(stats, "tp", 0, 0, tiled=True)
    groups = filter_mr.shape[0] // 8
    (
        grad_query_se, grad_key_mr, prod_mr, grad_conv_se, head, tiles, small
    ) = call(
        main_kernel,
        cols,
        [fixed(8, 8, 128)] + [wide(tokens)] * 3 + [wide(2 * tokens)] + [wide(tokens)] * 4
        + [wide(HALO), wide(1)] + mats[1:],
        [wide(tokens)] * 4
        + [wide(HALO), pl.BlockSpec((groups, WIDTH // 128, 8, 128), lambda i: (0, i, 0, 0))]
        + [wide(se_taps + 1)],
        [(full, BF16)] * 4
        + [((HALO, cols), BF16), ((groups, cols // 128, 8, 128), BF16), ((se_taps + 1, cols), F32)],
        [pltpu.VMEM((tokens + HALO, WIDTH), F32)] + [pltpu.VMEM((tokens, 128), F32)] * 2,
        2000 * tokens * cols,
        40 * tokens * cols,
    )(
        stats, mixed_se, conv_se, grad_prod_mr, spectrum, key_mr, query_se, key_se, value_path,
        rim_se, gain, half, back_first,
    )
    rim_mr = shifted(prod_mr, "ctx", 1)
    rim_grad_se = shifted(head, "ctx", -1)
    grad_filter_mr, small = filter_totals(tiles, small)
    grad_query_mr, grad_key_se, grad_value = call(
        last_kernel,
        cols,
        [wide(tokens)] * 5 + [wide(HALO), wide(se_taps)] + [wide(tokens)] * 2 + mats,
        [wide(tokens)] * 3,
        [(full, BF16)] * 3,
        [pltpu.VMEM((tokens + HALO, WIDTH), F32)],
        3000 * tokens * cols,
        20 * tokens * cols,
    )(
        prod_mr, rim_mr, out_grad, filter_mr, grad_conv_se, rim_grad_se, filter_se, value_path,
        key_se, whole, half, back_last,
    )
    return (
        grad_value,
        grad_query_se,
        grad_key_se,
        grad_query_mr,
        grad_key_mr,
        small[:se_taps],
        grad_filter_mr,
        small[se_taps],
    )


def solution(mesh):
    spread = P("ctx", "tp")
    return jax.shard_map(
        shards,
        mesh=mesh,
        in_specs=(spread,) * 6 + (P("tp"), P(None, "tp"), P(None, "tp")),
        out_specs=(spread,) * 5 + (P(None, "tp"), P(None, "tp"), P("tp")),
        check_vma=False,
    )
```

time: 134 us -> 105 us (0.78)
  the two profiles are of different devices: /device:TPU:2 before, /device:TPU:128 now
where the time goes in v2:
time: 105 us
  blocking collectives  47.2 us (45%)
  starting transfers between devices  25.8 us (25%)
  waiting for transfers between devices  13.8 us (13%)
  Pallas kernels  11.1 us (11%)
  local copies, waits for them, and re-layouts  3.38 us (3%)
  other arithmetic  2.66 us (3%)
    all_to_all x1, blocking collectives, filter_totals(): got = lax.all_to_all(packed, 'ctx', 0, 0, tiled=True)  23.7 us
    all_to_all x1, blocking collectives, shards(): stats = lax.all_to_all(stats, 'tp', 0, 0, tiled=True)  23.5 us
    ppermute x4, starting transfers between devices, shifted(): return lax.ppermute(block, axis, route)  18.8 us
    ppermute x4, waiting for transfers between devices, shifted(): return lax.ppermute(block, axis, route)  13.8 us
    all_to_all x1, starting transfers between devices, filter_totals(): back = lax.all_to_all(spread, 'ctx', 0, 0, tiled=True)  7 us
    pallas_call x1, Pallas kernels, shards(): call(main_kernel, cols, [fixed(8, 8, 128)] + [wide(tokens)] * 3 + [wide(2...  3.84 us
    pallas_call x1, Pallas kernels, shards(): call(last_kernel, cols, [wide(tokens)] * 5 + [wide(HALO), wide(se_taps)]...  3.57 us
    pallas_call x1, Pallas kernels, shards(): call(dot_kernel, cols, [wide(tokens)] * 4 + [wide(1), wide(tokens), fixed...  2.68 us
  transfers between devices with their start and end apart: 5, of which 3 were waited for; matrix products, arithmetic and copies ran while one was open for 0% of the time, Pallas kernels for 4%

profile of v2, /device:TPU:128, one launch (start us, length us, event | category | flops | bytes accessed | tf_op | source)
XLA Modules:
  0.0 104.9 jit_solution(7734034577970415224)
XLA Ops:
  0.6 0.0 copy-start
  0.6 0.0 copy-start.1
  0.7 0.0 copy-start.4
  0.7 0.0 copy-start.11
  0.7 1.2 %multiply_convert_fusion.grad = bf16[128,1024]{1,0:T(8,128)(2,1)S(1)} fusion(bf16[128,1024]{1,0:T(8,128)(2,1)} %param.17, bf16[128,1024]{1,0:T(8,128)(2,1)} %out_grad.1), kind=kLoop, calls=%fused_computation.3 | loop fusion | flops 524288 | bytes 786432 | tf_op jit(solution)/shard_map/convert_element_type | solution.py:223
  1.8 0.0 copy-start.12
  1.9 6.7 %collective-permute-start = (bf16[128,1024]{1,0:T(8,128)(2,1)S(1)}, bf16[128,1024]{1,0:T(8,128)(2,1)S(1)}, u32[]{:S(2)}, u32[]{:S(2)}) collective-permute-start(bf16[128,1024]{1,0:T(8,128)(2,1)S(1)} %multiply_convert_fusion.grad), channel_id=1, source_target_pairs={{8,0},{16,8},{24,16},{32,24},{40,32},{48,40},{56,48},{64,56},{72,6... | collective-permute-start | bytes 786440 | tf_op jit(solution)/shard_map/ppermute | solution.py:196
  8.5 0.0 copy-done
  8.5 0.0 copy-done.1
  8.5 0.0 copy-start.7
  8.6 2.1 %collective-permute-start.1 = (bf16[16,1024]{1,0:T(8,128)(2,1)S(1)}, bf16[16,1024]{1,0:T(8,128)(2,1)S(1)}, u32[]{:S(2)}, u32[]{:S(2)}) collective-permute-start(bf16[16,1024]{1,0:T(8,128)(2,1)S(1)} %multiply_convert_fusion.1), channel_id=1, source_target_pairs={{0,8},{8,16},{16,24},{24,32},{32,40},{40,48},{48,56},{56,64},{64,7... | collective-permute-start | bytes 98312 | tf_op jit(solution)/shard_map/ppermute | solution.py:196
  10.6 0.0 copy-done.12
  10.7 0.0 copy-start.2
  10.7 0.0 copy-start.3
  10.7 0.0 copy-start.6
  10.7 8.0 %collective-permute-done.1.rim = bf16[16,1024]{1,0:T(8,128)(2,1)S(1)} collective-permute-done((bf16[16,1024]{1,0:T(8,128)(2,1)S(1)}, bf16[16,1024]{1,0:T(8,128)(2,1)S(1)}, u32[]{:S(2)}, u32[]{:S(2)}) %collective-permute-start.1) | collective-permute-done | bytes 32800 | tf_op jit(solution)/shard_map/ppermute | solution.py:196
  18.7 0.0 copy-done.4
  18.7 0.0 copy-done.11
  18.7 1.0 shard_map.188
  19.7 0.0 collective-permute-done.rim
  19.8 0.0 copy-done.7
  19.8 0.0 copy-done.2
  19.8 0.0 copy-done.3
  19.8 0.0 copy-done.6
  19.8 0.0 copy-start.8
  19.8 0.9 copy-done.8
  20.7 0.0 copy-start.9
  20.7 2.7 %shard_map.189 = (f32[128,1024]{1,0:T(8,128)S(1)}, f32[256,1024]{1,0:T(8,128)S(1)}, f32[8,8,128]{2,1,0:T(8,128)S(1)}) custom-call(bf16[128,1024]{1,0:T(8,128)(2,1)S(1)} %multiply_convert_fusion.grad, bf16[128,1024]{1,0:T(8,128)(2,1)S(1)} %collective-permute-done.rim, bf16[128,1024]{1,0:T(8,128)(2,1)S(1)} %copy-done.6, bf16[128,1024]{1,0:T(8,128)(2,1)S(1)} %copy-done.3, ...), custom_call_target="tpu_custom_call" | custom-call | flops 393216000 | bytes 3145728 | tf_op jit(solution)/shard_map/pallas_call | solution.py:237
  23.4 23.5 %all_to_all.15.stats = f32[8,8,128]{2,1,0:T(8,128)S(1)} all-to-all(f32[8,8,128]{2,1,0:T(8,128)S(1)} %get-tuple-element.26), channel_id=1, replica_groups=mesh['ctx'=128,'tp'=8] {'tp'}, dimensions={0} | all-to-all | bytes 65536 | tf_op jit(solution)/shard_map/all_to_all | solution.py:247
  46.9 0.0 copy-done.9
  46.9 3.8 %shard_map.190 = (bf16[128,1024]{1,0:T(8,128)(2,1)}, bf16[128,1024]{1,0:T(8,128)(2,1)}, bf16[128,1024]{1,0:T(8,128)(2,1)S(1)}, bf16[128,1024]{1,0:T(8,128)(2,1)S...) custom-call(f32[8,8,128]{2,1,0:T(8,128)S(1)} %all_to_all.15.stats, ...), custom_call_target="tpu_custom_call" | custom-call | flops 262144000 | bytes 5242880 | tf_op jit(solution)/shard_map/pallas_call | solution.py:251
  50.8 0.3 fusion
  51.1 23.7 %all_to_all.16 = bf16[128,5,2,128]{3,2,1,0:T(2,128)(2,1)S(1)} all-to-all(bf16[128,5,2,128]{3,2,1,0:T(2,128)(2,1)S(1)} %fusion), channel_id=1, replica_groups=mesh['ctx'=128,'tp'=8] {'ctx'}, dimensions={0} | all-to-all | bytes 655360 | tf_op jit(solution)/shard_map/all_to_all | solution.py:205
  74.8 0.3 convert_reduce_fusion
  75.1 0.9 broadcast_in_dim.2
  76.0 0.0 copy-start.5
  76.0 0.0 copy-start.10
  76.0 7.0 %all-to-all-start.2 = ((bf16[128,5,2,128]{3,2,1,0:T(2,128)(2,1)}), bf16[128,5,2,128]{3,2,1,0:T(2,128)(2,1)S(1)}, u32[]{:S(2)}, u32[]{:S(2)}) async-start(bf16[128,5,2,128]{3,2,1,0:T(2,128)(2,1)} %broadcast_in_dim.2), calls=%async_computation.2 | async-start | bytes 655360 | tf_op jit(solution)/shard_map/all_to_all | solution.py:208
  83.1 3.4 %collective-permute-start.2 = (bf16[128,1024]{1,0:T(8,128)(2,1)S(1)}, bf16[128,1024]{1,0:T(8,128)(2,1)S(1)}, u32[]{:S(2)}, u32[]{:S(2)}) collective-permute-start(bf16[128,1024]{1,0:T(8,128)(2,1)S(1)} %get-tuple-element.30.prod_mr), channel_id=1, source_target_pairs={{0,8},{8,16},{16,24},{24,32},{32,40},{40,48},{48,56},{56,64},{64,7... | collective-permute-start | bytes 786440 | tf_op jit(solution)/shard_map/ppermute | solution.py:196
  86.4 6.7 %collective-permute-start.3 = (bf16[16,1024]{1,0:T(8,128)(2,1)S(1)}, bf16[16,1024]{1,0:T(8,128)(2,1)S(1)}, u32[]{:S(2)}, u32[]{:S(2)}) collective-permute-start(bf16[16,1024]{1,0:T(8,128)(2,1)S(1)} %get-tuple-element.32), channel_id=1, source_target_pairs={{8,0},{16,8},{24,16},{32,24},{40,32},{48,40},{56,48},{64,56},{72,6... | collective-permute-start | bytes 98312 | tf_op jit(solution)/shard_map/ppermute | solution.py:196
  93.1 1.6 %collective-permute-done.3.rim_se = bf16[16,1024]{1,0:T(8,128)(2,1)S(1)} collective-permute-done((bf16[16,1024]{1,0:T(8,128)(2,1)S(1)}, bf16[16,1024]{1,0:T(8,128)(2,1)S(1)}, u32[]{:S(2)}, u32[]{:S(2)}) %collective-permute-start.3) | collective-permute-done | bytes 32800 | tf_op jit(solution)/shard_map/ppermute | solution.py:196
  94.7 4.2 %collective-permute-done.2.rim_mr = bf16[128,1024]{1,0:T(8,128)(2,1)S(1)} collective-permute-done((bf16[128,1024]{1,0:T(8,128)(2,1)S(1)}, bf16[128,1024]{1,0:T(8,128)(2,1)S(1)}, u32[]{:S(2)}, u32[]{:S(2)}) %collective-permute-start.2) | collective-permute-done | bytes 262176 | tf_op jit(solution)/shard_map/ppermute | solution.py:196
  98.9 0.0 copy-done.5
  98.9 0.0 copy-done.10
  98.9 3.6 %shard_map.191 = (bf16[128,1024]{1,0:T(8,128)(2,1)}, bf16[128,1024]{1,0:T(8,128)(2,1)}, bf16[128,1024]{1,0:T(8,128)(2,1)}) custom-call(bf16[128,1024]{1,0:T(8,128)(2,1)S(1)} %get-tuple-element.30.prod_mr, bf16[128,1024]{1,0:T(8,128)(2,1)S(1)} %collective-permute-done.2.rim_mr, bf16[128,1024]{1,0:T(8,128)(2,1)S(1)} %copy-done.5, ...), custom_call_target="tpu_custom_call" | custom-call | flops 393216000 | bytes 2621440 | tf_op jit(solution)/shard_map/pallas_call | solution.py:271
  102.5 0.0 all-to-all-done.2
  102.5 0.6 slice.34
  103.1 0.1 slice_reduce_fusion
  103.2 0.6 slice.28
  103.8 0.2 slice.33
  104.0 0.8 convert_bitcast_fusion
  (5 shorter events, 0.1 us)
Async XLA Ops:
  0.6 7.9 %copy-start = (bf16[128,1024]{1,0:T(8,128)(2,1)S(1)}, bf16[128,1024]{1,0:T(8,128)(2,1)}, u32[]{:S(2)}) copy-start(bf16[128,1024]{1,0:T(8,128)(2,1)} %key_se.3) | copy-start | bytes 786436
  0.6 7.9 %copy-start.1 = (bf16[128,1024]{1,0:T(8,128)(2,1)S(1)}, bf16[128,1024]{1,0:T(8,128)(2,1)}, u32[]{:S(2)}) copy-start(bf16[128,1024]{1,0:T(8,128)(2,1)} %value.5) | copy-start | bytes 786436
  0.7 18.1 %copy-start.4 = (bf16[128,1024]{1,0:T(8,128)(2,1)S(1)}, bf16[128,1024]{1,0:T(8,128)(2,1)}, u32[]{:S(2)}) copy-start(bf16[128,1024]{1,0:T(8,128)(2,1)} %query_se.1) | copy-start | bytes 786436
  0.7 18.1 %copy-start.11 = (bf16[7,1024]{1,0:T(8,128)(2,1)S(1)}, bf16[7,1024]{1,0:T(8,128)(2,1)}, u32[]{:S(2)}) copy-start(bf16[7,1024]{1,0:T(8,128)(2,1)} %taps_se.1) | copy-start | bytes 43012
  1.8 8.8 %copy-start.12 = (bf16[1024]{0:T(1024)(128)(2,1)S(1)}, bf16[1024]{0:T(1024)(128)(2,1)}, u32[]{:S(2)}) copy-start(bf16[1024]{0:T(1024)(128)(2,1)} %param.19) | copy-start | bytes 6148
  1.9 17.9 %collective-permute-start = (bf16[128,1024]{1,0:T(8,128)(2,1)S(1)}, bf16[128,1024]{1,0:T(8,128)(2,1)S(1)}, u32[]{:S(2)}, u32[]{:S(2)}) collective-permute-start(bf16[128,1024]{1,0:T(8,128)(2,1)S(1)} %multiply_convert_fusion.grad), channel_id=1, source_target_pairs={{8,0},{16,8},{24,16},{32,24},{40,32},{48,40},{56,48},{64,56},{72,6... | collective-permute-start | bytes 786440 | tf_op jit(solution)/shard_map/ppermute | solution.py:196
  8.5 11.2 %copy-start.7 = (bf16[256,512]{1,0:T(8,128)(2,1)S(1)}, bf16[256,512]{1,0:T(8,128)(2,1)}, u32[]{:S(2)}) copy-start(bf16[256,512]{1,0:T(8,128)(2,1)} %constant.13.clone.whole) | copy-start | bytes 786436
  8.6 10.2 %collective-permute-start.1 = (bf16[16,1024]{1,0:T(8,128)(2,1)S(1)}, bf16[16,1024]{1,0:T(8,128)(2,1)S(1)}, u32[]{:S(2)}, u32[]{:S(2)}) collective-permute-start(bf16[16,1024]{1,0:T(8,128)(2,1)S(1)} %multiply_convert_fusion.1), channel_id=1, source_target_pairs={{0,8},{8,16},{16,24},{24,32},{32,40},{40,48},{48,56},{56,64},{64,7... | collective-permute-start | bytes 98312 | tf_op jit(solution)/shard_map/ppermute | solution.py:196
  10.7 9.1 %copy-start.2 = (bf16[256,256]{1,0:T(8,128)(2,1)S(1)}, bf16[256,256]{1,0:T(8,128)(2,1)}, u32[]{:S(2)}) copy-start(bf16[256,256]{1,0:T(8,128)(2,1)} %constant.14.clone.half) | copy-start | bytes 393220
  10.7 9.1 %copy-start.3 = (bf16[128,1024]{1,0:T(8,128)(2,1)S(1)}, bf16[128,1024]{1,0:T(8,128)(2,1)}, u32[]{:S(2)}) copy-start(bf16[128,1024]{1,0:T(8,128)(2,1)} %key_mr.1) | copy-start | bytes 786436
  10.7 9.1 %copy-start.6 = (bf16[128,1024]{1,0:T(8,128)(2,1)S(1)}, bf16[128,1024]{1,0:T(8,128)(2,1)}, u32[]{:S(2)}) copy-start(bf16[128,1024]{1,0:T(8,128)(2,1)} %taps_mr.1) | copy-start | bytes 786436
  19.8 0.9 copy-start.8
  20.7 26.2 %copy-start.9 = (bf16[128,768]{1,0:T(8,128)(2,1)S(1)}, bf16[128,768]{1,0:T(8,128)(2,1)}, u32[]{:S(2)}) copy-start(bf16[128,768]{1,0:T(8,128)(2,1)} %constant.15.clone.back) | copy-start | bytes 589828
  76.0 22.9 %copy-start.5 = (bf16[128,1024]{1,0:T(8,128)(2,1)S(1)}, bf16[128,1024]{1,0:T(8,128)(2,1)}, u32[]{:S(2)}) copy-start(bf16[128,1024]{1,0:T(8,128)(2,1)} %out_grad.1) | copy-start | bytes 786436
  76.0 22.9 %copy-start.10 = (bf16[128,768]{1,0:T(8,128)(2,1)S(1)}, bf16[128,768]{1,0:T(8,128)(2,1)}, u32[]{:S(2)}) copy-start(bf16[128,768]{1,0:T(8,128)(2,1)} %constant.16.clone.back) | copy-start | bytes 589828
  76.0 26.5 %all-to-all-start.2 = ((bf16[128,5,2,128]{3,2,1,0:T(2,128)(2,1)}), bf16[128,5,2,128]{3,2,1,0:T(2,128)(2,1)S(1)}, u32[]{:S(2)}, u32[]{:S(2)}) async-start(bf16[128,5,2,128]{3,2,1,0:T(2,128)(2,1)} %broadcast_in_dim.2), calls=%async_computation.2 | async-start | bytes 655360 | tf_op jit(solution)/shard_map/all_to_all | solution.py:208
  83.1 15.9 %collective-permute-start.2 = (bf16[128,1024]{1,0:T(8,128)(2,1)S(1)}, bf16[128,1024]{1,0:T(8,128)(2,1)S(1)}, u32[]{:S(2)}, u32[]{:S(2)}) collective-permute-start(bf16[128,1024]{1,0:T(8,128)(2,1)S(1)} %get-tuple-element.30.prod_mr), channel_id=1, source_target_pairs={{0,8},{8,16},{16,24},{24,32},{32,40},{40,48},{48,56},{56,64},{64,7... | collective-permute-start | bytes 786440 | tf_op jit(solution)/shard_map/ppermute | solution.py:196
  86.4 8.3 %collective-permute-start.3 = (bf16[16,1024]{1,0:T(8,128)(2,1)S(1)}, bf16[16,1024]{1,0:T(8,128)(2,1)S(1)}, u32[]{:S(2)}, u32[]{:S(2)}) collective-permute-start(bf16[16,1024]{1,0:T(8,128)(2,1)S(1)} %get-tuple-element.32), channel_id=1, source_target_pairs={{8,0},{16,8},{24,16},{32,24},{40,32},{48,40},{56,48},{64,56},{72,6... | collective-permute-start | bytes 98312 | tf_op jit(solution)/shard_map/ppermute | solution.py:196

commit v3 on v2

--- a/solution.py
+++ b/solution.py
@@ -7,7 +7,7 @@
 from jax.sharding import PartitionSpec as P
 
 D = 8192
-WIDTH = 256
+WIDTH = 1024
 HALO = 16
 F32 = jnp.float32
 BF16 = jnp.bfloat16
@@ -27,8 +27,9 @@
     i_high, i_low = split(inverse)
     whole = np.concatenate([f_high, f_low], axis=1)
     half = np.concatenate([f_high[:, :128], f_low[:, :128]], axis=1)
+    later = np.concatenate([f_high[:, 128:], f_low[:, 128:]], axis=1)
     back = np.concatenate([i_high, i_high, i_low], axis=1)
-    return jnp.asarray(whole), jnp.asarray(half), jnp.asarray(back[:128]), jnp.asarray(back[128:])
+    return [jnp.asarray(m) for m in (whole, half, later, back[:128], back[128:])]
 
 
 def to_spectrum(matrix, *rows):
@@ -64,7 +65,11 @@
     win[HALO:] = prod.astype(F32)
 
 
-def se_kernel(key, value, query, rim, taps, conv, mixed, square, win):
+def se_kernel(
+    key, value, query, rim, taps, grad, taps_mr, half, conv, mixed, square, kernel, near, win
+):
+    kernel[...] = to_spectrum(half[...], taps_mr[...])
+    near[...] = to_spectrum(half[...], grad[...])
     se_window(win, rim, key, value)
     f = taps[...].astype(F32)
     total = f[0:1] * win[HALO : HALO + 128]
@@ -82,12 +87,11 @@
 
 
 def dot_kernel(
-    grad, rim, taps, key, gain, mixed, square, whole, half, back, prod, spectrum, stats, acc
-):
-    kernel = to_spectrum(half[...], taps[...])
-    signal = to_spectrum(whole[...], grad[...], rim[...])
+    near, rim, kernel, key, gain, mixed, square, later, back, prod, spectrum, stats, acc
+):
+    signal = near[...] + to_spectrum(later[...], rim[...])
     spectrum[...] = signal
-    gp = correlated(back[...], kernel, signal)
+    gp = correlated(back[...], kernel[...], signal)
     prod[...] = gp
     scaled = gp * key[...].astype(F32) * gain[...].astype(F32)
 
@@ -152,12 +156,11 @@
 
 
 def last_kernel(
-    prod_mr, rim_mr, out_grad, taps_mr, conv_se, rim_se, taps_se, value, key_se, whole, half, back,
+    prod_mr, rim_mr, out_grad, kernel, conv_se, rim_se, taps_se, value, key_se, whole, back,
     out_query_mr, out_key_se, out_value, win,
 ):
-    kernel = to_spectrum(half[...], taps_mr[...])
     signal = to_spectrum(whole[...], rim_mr[...], prod_mr[...])
-    conv = convolved(back[...], kernel, signal)
+    conv = convolved(back[...], kernel[...], signal)
     out_query_mr[...] = (out_grad[...].astype(F32) * conv).astype(BF16)
     win[0:128] = conv_se[...].astype(F32)
     win[128:] = rim_se[...].astype(F32)
@@ -167,6 +170,10 @@
         total = total + f[j : j + 1] * win[j : j + 128]
     out_key_se[...] = (total * value[...].astype(F32)).astype(BF16)
     out_value[...] = (total * key_se[...].astype(F32)).astype(BF16)
+
+
+def gate_kernel(got, rim_mr, rim_se, out):
+    del got, rim_mr, rim_se, out
 
 
 def wide(rows):
@@ -196,19 +203,27 @@
     return lax.ppermute(block, axis, route)
 
 
-def filter_totals(tiles, small):
+def filter_totals(tiles, small, rims):
     n = lax.axis_size("ctx")
     cols = small.shape[1]
-    rows = small.reshape(-1, 1, 1, 128).astype(BF16)
+    rows = small.reshape(8, -1, 128).transpose(1, 0, 2).reshape(-1, 1, 1, 128).astype(BF16)
     rows = jnp.pad(rows, ((0, n - rows.shape[0]), (0, 0), (0, 1), (0, 0)))
     packed = jnp.concatenate([tiles.reshape(n, 4, 2, 128), rows], axis=1)
     got = lax.all_to_all(packed, "ctx", 0, 0, tiled=True)
+    anywhere = pl.BlockSpec(memory_space=pl.ANY)
+    got = pl.pallas_call(
+        gate_kernel,
+        in_specs=[anywhere] * 3,
+        out_specs=anywhere,
+        out_shape=jax.ShapeDtypeStruct(got.shape, BF16),
+        input_output_aliases={0: 0},
+    )(got, *rims)
     total = lax.optimization_barrier(jnp.sum(got.astype(F32), axis=0)).astype(BF16)
     spread = jnp.broadcast_to(total[None], (n,) + total.shape)
     back = lax.all_to_all(spread, "ctx", 0, 0, tiled=True)
     mr_sum = back[:, :4].reshape(tiles.shape).astype(F32).transpose(0, 2, 1, 3).reshape(-1, cols)
-    small_sum = back[: cols // 16, 4, 0].astype(F32).reshape(8, cols)
-    return mr_sum, small_sum
+    small_sum = back[: cols // 16, 4, 0].astype(F32).reshape(-1, 8, 128)
+    return mr_sum, small_sum.transpose(1, 0, 2).reshape(8, cols)
 
 
 def shards(
@@ -217,33 +232,35 @@
     tokens, cols = value_path.shape
     se_taps = filter_se.shape[0]
     full = (tokens, cols)
-    whole, half, back_first, back_last = transforms()
+    whole, half, later, back_first, back_last = transforms()
     gain = norm_gain.reshape(1, cols)
     tail = (key_se[-HALO:].astype(F32) * value_path[-HALO:].astype(F32)).astype(BF16)
     grad_conv_mr = (out_grad.astype(F32) * query_mr.astype(F32)).astype(BF16)
     rim_se = shifted(tail, "ctx", 1)
     rim_grad_mr = shifted(grad_conv_mr, "ctx", -1)
-    mats = [fixed(*whole.shape), fixed(*half.shape), fixed(*back_first.shape)]
-    conv_se, mixed_se, square = call(
+    half_spec, back_spec = fixed(*half.shape), fixed(*back_first.shape)
+    spectral = (2 * tokens, cols)
+    conv_se, mixed_se, square, kernel_mr, near = call(
         se_kernel,
         cols,
-        [wide(tokens)] * 3 + [wide(HALO), wide(se_taps)],
-        [wide(tokens), wide(tokens), fixed(tokens, 128)],
-        [(full, F32), (full, F32), ((tokens, 128), F32)],
+        [wide(tokens)] * 3 + [wide(HALO), wide(se_taps)] + [wide(tokens)] * 2 + [half_spec],
+        [wide(tokens), wide(tokens), fixed(tokens, 128)] + [wide(2 * tokens)] * 2,
+        [(full, F32), (full, F32), ((tokens, 128), F32), (spectral, F32), (spectral, F32)],
         [pltpu.VMEM((tokens + HALO, WIDTH), F32)],
-        18 * tokens * cols,
+        2000 * tokens * cols,
         14 * tokens * cols,
-    )(key_se, value_path, query_se, rim_se, filter_se)
+    )(key_se, value_path, query_se, rim_se, filter_se, grad_conv_mr, filter_mr, half)
     grad_prod_mr, spectrum, stats = call(
         dot_kernel,
         cols,
-        [wide(tokens)] * 4 + [wide(1), wide(tokens), fixed(tokens, 128)] + mats,
+        [wide(2 * tokens), wide(tokens), wide(2 * tokens), wide(tokens), wide(1), wide(tokens)]
+        + [fixed(tokens, 128), half_spec, back_spec],
         [wide(tokens), wide(2 * tokens), fixed(8, 8, 128)],
-        [(full, F32), ((2 * tokens, cols), F32), ((8, 8, 128), F32)],
+        [(full, F32), (spectral, F32), ((8, 8, 128), F32)],
         [pltpu.VMEM((tokens, 128), F32)],
         3000 * tokens * cols,
         24 * tokens * cols,
-    )(grad_conv_mr, rim_grad_mr, filter_mr, key_mr, gain, mixed_se, square, whole, half, back_first)
+    )(near, rim_grad_mr, kernel_mr, key_mr, gain, mixed_se, square, later, back_first)
     stats = lax.all_to_all(stats, "tp", 0, 0, tiled=True)
     groups = filter_mr.shape[0] // 8
     (
@@ -252,7 +269,7 @@
         main_kernel,
         cols,
         [fixed(8, 8, 128)] + [wide(tokens)] * 3 + [wide(2 * tokens)] + [wide(tokens)] * 4
-        + [wide(HALO), wide(1)] + mats[1:],
+        + [wide(HALO), wide(1), half_spec, back_spec],
         [wide(tokens)] * 4
         + [wide(HALO), pl.BlockSpec((groups, WIDTH // 128, 8, 128), lambda i: (0, i, 0, 0))]
         + [wide(se_taps + 1)],
@@ -267,19 +284,20 @@
     )
     rim_mr = shifted(prod_mr, "ctx", 1)
     rim_grad_se = shifted(head, "ctx", -1)
-    grad_filter_mr, small = filter_totals(tiles, small)
+    grad_filter_mr, small = filter_totals(tiles, small, (rim_mr, rim_grad_se))
     grad_query_mr, grad_key_se, grad_value = call(
         last_kernel,
         cols,
-        [wide(tokens)] * 5 + [wide(HALO), wide(se_taps)] + [wide(tokens)] * 2 + mats,
+        [wide(tokens)] * 3 + [wide(2 * tokens), wide(tokens), wide(HALO), wide(se_taps)]
+        + [wide(tokens)] * 2 + [fixed(*whole.shape), back_spec],
         [wide(tokens)] * 3,
         [(full, BF16)] * 3,
         [pltpu.VMEM((tokens + HALO, WIDTH), F32)],
         3000 * tokens * cols,
         20 * tokens * cols,
     )(
-        prod_mr, rim_mr, out_grad, filter_mr, grad_conv_se, rim_grad_se, filter_se, value_path,
-        key_se, whole, half, back_last,
+        prod_mr, rim_mr, out_grad, kernel_mr, grad_conv_se, rim_grad_se, filter_se, value_path,
+        key_se, whole, back_last,
     )
     return (
         grad_value,

time: 105 us -> 109 us (1.038)
  the two profiles are of different devices: /device:TPU:128 before, /device:TPU:2 now
where the time goes in v3:
time: 109 us
  starting transfers between devices  51.3 us (47%)
  waiting for transfers between devices  29.5 us (27%)
  blocking collectives  10.8 us (10%)
  Pallas kernels  6.59 us (6%)
  local copies, waits for them, and re-layouts  5.01 us (5%)
  other arithmetic  4.35 us (4%)
    ppermute x4, starting transfers between devices, shifted(): return lax.ppermute(block, axis, route)  22.9 us
    all_to_all x1, starting transfers between devices, filter_totals(): got = lax.all_to_all(packed, 'ctx', 0, 0, tiled=True)  17.4 us
    all_to_all x1, waiting for transfers between devices, filter_totals(): back = lax.all_to_all(spread, 'ctx', 0, 0, tiled=True)  14.3 us
    all_to_all x1, starting transfers between devices, filter_totals(): back = lax.all_to_all(spread, 'ctx', 0, 0, tiled=True)  11.1 us
    ppermute x4, waiting for transfers between devices, shifted(): return lax.ppermute(block, axis, route)  11.1 us
    all_to_all x1, blocking collectives, shards(): stats = lax.all_to_all(stats, 'tp', 0, 0, tiled=True)  10.8 us
    all_to_all x1, waiting for transfers between devices, filter_totals(): got = lax.all_to_all(packed, 'ctx', 0, 0, tiled=True)  4.08 us
    unnamed x38, local copies, waits for them, and re-layouts  2.66 us
  transfers between devices with their start and end apart: 6, of which 5 were waited for; matrix products, arithmetic and copies ran while one was open for 0% of the time, Pallas kernels for 3%

profile of v3, /device:TPU:2, one launch (start us, length us, event | category | flops | bytes accessed | tf_op | source)
XLA Modules:
  0.0 108.5 jit_solution(11593877606984660752)
XLA Ops:
  0.6 0.0 copy-start
  0.6 0.0 copy-start.1
  0.7 0.0 copy-start.3
  0.7 1.2 %multiply_convert_fusion.grad = bf16[128,1024]{1,0:T(8,128)(2,1)S(1)} fusion(bf16[128,1024]{1,0:T(8,128)(2,1)} %param.18, bf16[128,1024]{1,0:T(8,128)(2,1)} %out_grad.1), kind=kLoop, calls=%fused_computation.3 | loop fusion | flops 524288 | bytes 786432 | tf_op jit(solution)/shard_map/convert_element_type | solution.py:238
  1.8 0.0 copy-start.18
  1.8 15.1 %collective-permute-start.1 = (bf16[128,1024]{1,0:T(8,128)(2,1)S(1)}, bf16[128,1024]{1,0:T(8,128)(2,1)S(1)}, u32[]{:S(2)}, u32[]{:S(2)}) collective-permute-start(bf16[128,1024]{1,0:T(8,128)(2,1)S(1)} %multiply_convert_fusion.grad), channel_id=1, source_target_pairs={{8,0},{16,8},{24,16},{32,24},{40,32},{48,40},{56,48},{64,56},{72,6... | collective-permute-start | bytes 786440 | tf_op jit(solution)/shard_map/ppermute | solution.py:203
  16.9 0.0 copy-done
  17.0 0.0 copy-done.1
  17.0 0.0 copy-start.16
  17.0 1.9 %collective-permute-start = (bf16[16,1024]{1,0:T(8,128)(2,1)S(1)}, bf16[16,1024]{1,0:T(8,128)(2,1)S(1)}, u32[]{:S(2)}, u32[]{:S(2)}) collective-permute-start(bf16[16,1024]{1,0:T(8,128)(2,1)S(1)} %multiply_convert_fusion.1), channel_id=1, source_target_pairs={{0,8},{8,16},{16,24},{24,32},{32,40},{40,48},{48,56},{56,64},{64,7... | collective-permute-start | bytes 98312 | tf_op jit(solution)/shard_map/ppermute | solution.py:203
  18.9 0.0 copy-done.18
  18.9 0.0 copy-start.6
  19.0 0.0 copy-start.7
  19.0 3.8 %collective-permute-done.rim = bf16[16,1024]{1,0:T(8,128)(2,1)S(1)} collective-permute-done((bf16[16,1024]{1,0:T(8,128)(2,1)S(1)}, bf16[16,1024]{1,0:T(8,128)(2,1)S(1)}, u32[]{:S(2)}, u32[]{:S(2)}) %collective-permute-start) | collective-permute-done | bytes 32800 | tf_op jit(solution)/shard_map/ppermute | solution.py:203
  22.8 0.0 copy-done.3
  22.8 0.0 copy-done.16
  22.8 0.0 copy-start.8
  22.8 0.9 copy-done.8
  23.7 0.0 copy-start.11
  23.7 0.9 copy-done.11
  24.7 0.0 copy-start.13
  24.7 1.4 %shard_map.197 = (f32[128,1024]{1,0:T(8,128)S(1)}, f32[128,1024]{1,0:T(8,128)S(1)}, f32[128,128]{1,0:T(8,128)S(1)}, f32[256,1024]{1,0:T(8,128)S(1)}, f32[256,1024]{1,0:T(8,128)S(1)}) custom-call(bf16[128,1024]{1,0:T(8,128)(2,1)S(1)} %copy-done, bf16[128,1024]{1,0:T(8,128)(2,1)S(1)} %copy-done.1, bf16[128,1024]{1,0:T(8,128)(2,1)S(1)} %copy-done.3, ...), custom_call_target="tpu_custom_call" | custom-call | flops 262144000 | bytes 1835008 | tf_op jit(solution)/shard_map/pallas_call | solution.py:243
  26.0 0.0 collective-permute-done.1.rim
  26.0 0.0 copy-done.6
  26.1 0.0 copy-done.7
  26.1 0.0 copy-done.13
  26.1 0.0 copy-start.9
  26.1 0.9 shard_map.198
  27.0 10.8 %all_to_all.15.stats = f32[8,8,128]{2,1,0:T(8,128)S(1)} all-to-all(f32[8,8,128]{2,1,0:T(8,128)S(1)} %get-tuple-element.30), channel_id=1, replica_groups=mesh['ctx'=128,'tp'=8] {'tp'}, dimensions={0} | all-to-all | bytes 65536 | tf_op jit(solution)/shard_map/all_to_all | solution.py:264
  37.9 0.0 copy-done.9
  37.9 1.9 %shard_map.199 = (bf16[128,1024]{1,0:T(8,128)(2,1)}, bf16[128,1024]{1,0:T(8,128)(2,1)}, bf16[128,1024]{1,0:T(8,128)(2,1)S(1)}, bf16[128,1024]{1,0:T(8,128)(2,1)S...) custom-call(f32[8,8,128]{2,1,0:T(8,128)S(1)} %all_to_all.15.stats, ...), custom_call_target="tpu_custom_call" | custom-call | flops 262144000 | bytes 5242880 | tf_op jit(solution)/shard_map/pallas_call | solution.py:268
  39.8 1.0 fusion
  40.9 17.4 %all-to-all-start.1 = ((bf16[128,5,2,128]{3,2,1,0:T(2,128)(2,1)}), bf16[128,5,2,128]{3,2,1,0:T(2,128)(2,1)S(1)}, u32[]{:S(2)}, u32[]{:S(2)}) async-start(bf16[128,5,2,128]{3,2,1,0:T(2,128)(2,1)} %fusion), calls=%async_computation.1 | async-start | bytes 655360 | tf_op jit(solution)/shard_map/all_to_all | solution.py:212
  58.2 3.4 %collective-permute-start.2 = (bf16[128,1024]{1,0:T(8,128)(2,1)S(1)}, bf16[128,1024]{1,0:T(8,128)(2,1)S(1)}, u32[]{:S(2)}, u32[]{:S(2)}) collective-permute-start(bf16[128,1024]{1,0:T(8,128)(2,1)S(1)} %get-tuple-element.34.prod_mr), channel_id=1, source_target_pairs={{0,8},{8,16},{16,24},{24,32},{32,40},{40,48},{48,56},{56,64},{64,7... | collective-permute-start | bytes 786440 | tf_op jit(solution)/shard_map/ppermute | solution.py:203
  61.6 2.5 %collective-permute-start.3 = (bf16[16,1024]{1,0:T(8,128)(2,1)S(1)}, bf16[16,1024]{1,0:T(8,128)(2,1)S(1)}, u32[]{:S(2)}, u32[]{:S(2)}) collective-permute-start(bf16[16,1024]{1,0:T(8,128)(2,1)S(1)} %get-tuple-element.36), channel_id=1, source_target_pairs={{8,0},{16,8},{24,16},{32,24},{40,32},{48,40},{56,48},{64,56},{72,6... | collective-permute-start | bytes 98312 | tf_op jit(solution)/shard_map/ppermute | solution.py:203
  64.1 3.4 %collective-permute-done.3.rim_se = bf16[16,1024]{1,0:T(8,128)(2,1)S(1)} collective-permute-done((bf16[16,1024]{1,0:T(8,128)(2,1)S(1)}, bf16[16,1024]{1,0:T(8,128)(2,1)S(1)}, u32[]{:S(2)}, u32[]{:S(2)}) %collective-permute-start.3) | collective-permute-done | bytes 32800 | tf_op jit(solution)/shard_map/ppermute | solution.py:203
  67.5 0.0 copy-start.14
  67.5 3.8 %collective-permute-done.2.rim_mr = bf16[128,1024]{1,0:T(8,128)(2,1)S(1)} collective-permute-done((bf16[128,1024]{1,0:T(8,128)(2,1)S(1)}, bf16[128,1024]{1,0:T(8,128)(2,1)S(1)}, u32[]{:S(2)}, u32[]{:S(2)}) %collective-permute-start.2) | collective-permute-done | bytes 262176 | tf_op jit(solution)/shard_map/ppermute | solution.py:203
  71.3 0.0 copy-start.4
  71.3 4.1 %all-to-all-done.1.got = bf16[128,5,2,128]{3,2,1,0:T(2,128)(2,1)S(1)} async-done(((bf16[128,5,2,128]{3,2,1,0:T(2,128)(2,1)}), bf16[128,5,2,128]{3,2,1,0:T(2,128)(2,1)S(1)}, u32[]{:S(2)}, u32[]{:S(2)}) %all-to-all-start.1) | async-done | bytes 327712 | tf_op jit(solution)/shard_map/all_to_all | solution.py:212
  75.4 0.0 copy-done.14
  75.4 0.0 copy-done.4
  75.4 0.0 copy-start.17
  75.4 0.7 copy-done.17
  76.2 0.0 copy-start.15
  76.2 1.3 %convert_reduce_fusion = bf16[5,2,128]{2,1,0:T(2,128)(2,1)S(1)} fusion(bf16[128,5,2,128]{3,2,1,0:T(2,128)(2,1)} %shard_map.201), kind=kLoop, calls=%fused_computation.1 | loop fusion | flops 326400 | bytes 330240 | tf_op jit(solution)/shard_map/reduce_sum | solution.py:221
  77.5 0.0 copy-start.10
  77.5 0.0 copy-start.12
  77.5 0.9 broadcast_in_dim.2
  78.4 0.0 copy-start.2
  78.4 0.0 copy-start.5
  78.4 11.1 %all-to-all-start.2 = ((bf16[128,5,2,128]{3,2,1,0:T(2,128)(2,1)}), bf16[128,5,2,128]{3,2,1,0:T(2,128)(2,1)S(1)}, u32[]{:S(2)}, u32[]{:S(2)}) async-start(bf16[128,5,2,128]{3,2,1,0:T(2,128)(2,1)} %broadcast_in_dim.2), calls=%async_computation.2 | async-start | bytes 655360 | tf_op jit(solution)/shard_map/all_to_all | solution.py:223
  89.5 0.0 copy-done.15
  89.5 0.0 copy-done.10
  89.5 0.0 copy-done.12
  89.5 0.0 copy-done.2
  89.5 0.0 copy-done.5
  89.5 2.4 %shard_map.200 = (bf16[128,1024]{1,0:T(8,128)(2,1)}, bf16[128,1024]{1,0:T(8,128)(2,1)}, bf16[128,1024]{1,0:T(8,128)(2,1)}) custom-call(bf16[128,1024]{1,0:T(8,128)(2,1)S(1)} %get-tuple-element.34.prod_mr, bf16[128,1024]{1,0:T(8,128)(2,1)S(1)} %copy-done.5, bf16[128,1024]{1,0:T(8,128)(2,1)S(1)} %copy-done.2, f32[256,1024]{1,0:T(8,128)S(1)} %get-tuple-element.27.kernel, ...), custom_call_target="tpu_custom_call" | custom-call | flops 393216000 | bytes 2621440 | tf_op jit(solution)/shard_map/pallas_call | solution.py:288
  91.9 14.3 %all-to-all-done.2 = bf16[128,5,2,128]{3,2,1,0:T(2,128)(2,1)S(1)} async-done(((bf16[128,5,2,128]{3,2,1,0:T(2,128)(2,1)}), bf16[128,5,2,128]{3,2,1,0:T(2,128)(2,1)S(1)}, u32[]{:S(2)}, u32[]{:S(2)}) %all-to-all-start.2) | async-done | bytes 327712 | tf_op jit(solution)/shard_map/all_to_all | solution.py:223
  106.3 0.6 slice.32
  106.9 0.6 slice_bitcast_fusion
  107.5 0.2 slice.31
  107.7 0.8 convert_bitcast_fusion
  (7 shorter events, 0.1 us)
Async XLA Ops:
  0.6 16.3 %copy-start = (bf16[128,1024]{1,0:T(8,128)(2,1)S(1)}, bf16[128,1024]{1,0:T(8,128)(2,1)}, u32[]{:S(2)}) copy-start(bf16[128,1024]{1,0:T(8,128)(2,1)} %key_se.3) | copy-start | bytes 786436
  0.6 16.3 %copy-start.1 = (bf16[128,1024]{1,0:T(8,128)(2,1)S(1)}, bf16[128,1024]{1,0:T(8,128)(2,1)}, u32[]{:S(2)}) copy-start(bf16[128,1024]{1,0:T(8,128)(2,1)} %value.5) | copy-start | bytes 786436
  0.7 22.2 %copy-start.3 = (bf16[128,1024]{1,0:T(8,128)(2,1)S(1)}, bf16[128,1024]{1,0:T(8,128)(2,1)}, u32[]{:S(2)}) copy-start(bf16[128,1024]{1,0:T(8,128)(2,1)} %query_se.1) | copy-start | bytes 786436
  1.8 17.1 %copy-start.18 = (bf16[1024]{0:T(1024)(128)(2,1)S(1)}, bf16[1024]{0:T(1024)(128)(2,1)}, u32[]{:S(2)}) copy-start(bf16[1024]{0:T(1024)(128)(2,1)} %param.20) | copy-start | bytes 6148
  1.8 24.2 %collective-permute-start.1 = (bf16[128,1024]{1,0:T(8,128)(2,1)S(1)}, bf16[128,1024]{1,0:T(8,128)(2,1)S(1)}, u32[]{:S(2)}, u32[]{:S(2)}) collective-permute-start(bf16[128,1024]{1,0:T(8,128)(2,1)S(1)} %multiply_convert_fusion.grad), channel_id=1, source_target_pairs={{8,0},{16,8},{24,16},{32,24},{40,32},{48,40},{56,48},{64,56},{72,6... | collective-permute-start | bytes 786440 | tf_op jit(solution)/shard_map/ppermute | solution.py:203
  17.0 5.8 %copy-start.16 = (bf16[7,1024]{1,0:T(8,128)(2,1)S(1)}, bf16[7,1024]{1,0:T(8,128)(2,1)}, u32[]{:S(2)}) copy-start(bf16[7,1024]{1,0:T(8,128)(2,1)} %taps_se.1) | copy-start | bytes 43012
  17.0 5.8 %collective-permute-start = (bf16[16,1024]{1,0:T(8,128)(2,1)S(1)}, bf16[16,1024]{1,0:T(8,128)(2,1)S(1)}, u32[]{:S(2)}, u32[]{:S(2)}) collective-permute-start(bf16[16,1024]{1,0:T(8,128)(2,1)S(1)} %multiply_convert_fusion.1), channel_id=1, source_target_pairs={{0,8},{8,16},{16,24},{24,32},{32,40},{40,48},{48,56},{56,64},{64,7... | collective-permute-start | bytes 98312 | tf_op jit(solution)/shard_map/ppermute | solution.py:203
  18.9 7.1 %copy-start.6 = (bf16[128,1024]{1,0:T(8,128)(2,1)S(1)}, bf16[128,1024]{1,0:T(8,128)(2,1)}, u32[]{:S(2)}) copy-start(bf16[128,1024]{1,0:T(8,128)(2,1)} %key_mr.1) | copy-start | bytes 786436
  19.0 7.1 %copy-start.7 = (bf16[128,768]{1,0:T(8,128)(2,1)S(1)}, bf16[128,768]{1,0:T(8,128)(2,1)}, u32[]{:S(2)}) copy-start(bf16[128,768]{1,0:T(8,128)(2,1)} %constant.18.clone.back) | copy-start | bytes 589828
  22.8 0.9 copy-start.8
  23.7 0.9 copy-start.11
  24.7 1.4 %copy-start.13 = (bf16[256,256]{1,0:T(8,128)(2,1)S(1)}, bf16[256,256]{1,0:T(8,128)(2,1)}, u32[]{:S(2)}) copy-start(bf16[256,256]{1,0:T(8,128)(2,1)} %constant.17.clone.later) | copy-start | bytes 393220
  26.1 11.8 %copy-start.9 = (bf16[256,256]{1,0:T(8,128)(2,1)S(1)}, bf16[256,256]{1,0:T(8,128)(2,1)}, u32[]{:S(2)}) copy-start(bf16[256,256]{1,0:T(8,128)(2,1)} %constant.16.clone.half) | copy-start | bytes 393220
  40.9 34.6 %all-to-all-start.1 = ((bf16[128,5,2,128]{3,2,1,0:T(2,128)(2,1)}), bf16[128,5,2,128]{3,2,1,0:T(2,128)(2,1)S(1)}, u32[]{:S(2)}, u32[]{:S(2)}) async-start(bf16[128,5,2,128]{3,2,1,0:T(2,128)(2,1)} %fusion), calls=%async_computation.1 | async-start | bytes 655360 | tf_op jit(solution)/shard_map/all_to_all | solution.py:212
  58.2 13.1 %collective-permute-start.2 = (bf16[128,1024]{1,0:T(8,128)(2,1)S(1)}, bf16[128,1024]{1,0:T(8,128)(2,1)S(1)}, u32[]{:S(2)}, u32[]{:S(2)}) collective-permute-start(bf16[128,1024]{1,0:T(8,128)(2,1)S(1)} %get-tuple-element.34.prod_mr), channel_id=1, source_target_pairs={{0,8},{8,16},{16,24},{24,32},{32,40},{40,48},{48,56},{56,64},{64,7... | collective-permute-start | bytes 786440 | tf_op jit(solution)/shard_map/ppermute | solution.py:203
  61.6 5.9 %collective-permute-start.3 = (bf16[16,1024]{1,0:T(8,128)(2,1)S(1)}, bf16[16,1024]{1,0:T(8,128)(2,1)S(1)}, u32[]{:S(2)}, u32[]{:S(2)}) collective-permute-start(bf16[16,1024]{1,0:T(8,128)(2,1)S(1)} %get-tuple-element.36), channel_id=1, source_target_pairs={{8,0},{16,8},{24,16},{32,24},{40,32},{48,40},{56,48},{64,56},{72,6... | collective-permute-start | bytes 98312 | tf_op jit(solution)/shard_map/ppermute | solution.py:203
  67.5 7.9 %copy-start.14 = (bf16[16,1024]{1,0:T(8,128)(2,1)}, bf16[16,1024]{1,0:T(8,128)(2,1)S(1)}, u32[]{:S(2)}) copy-start(bf16[16,1024]{1,0:T(8,128)(2,1)S(1)} %collective-permute-done.3.rim_se) | copy-start | bytes 98308
  71.3 4.1 %copy-start.4 = (bf16[128,1024]{1,0:T(8,128)(2,1)}, bf16[128,1024]{1,0:T(8,128)(2,1)S(1)}, u32[]{:S(2)}) copy-start(bf16[128,1024]{1,0:T(8,128)(2,1)S(1)} %collective-permute-done.2.rim_mr) | copy-start | bytes 786436
  75.4 0.7 copy-start.17
  76.2 13.3 %copy-start.15 = (bf16[16,1024]{1,0:T(8,128)(2,1)S(1)}, bf16[16,1024]{1,0:T(8,128)(2,1)}, u32[]{:S(2)}) copy-start(bf16[16,1024]{1,0:T(8,128)(2,1)} %copy-done.14) | copy-start | bytes 98308
  77.5 12.0 %copy-start.10 = (bf16[256,512]{1,0:T(8,128)(2,1)S(1)}, bf16[256,512]{1,0:T(8,128)(2,1)}, u32[]{:S(2)}) copy-start(bf16[256,512]{1,0:T(8,128)(2,1)} %constant.15.clone.whole) | copy-start | bytes 786436
  77.5 12.0 %copy-start.12 = (bf16[128,768]{1,0:T(8,128)(2,1)S(1)}, bf16[128,768]{1,0:T(8,128)(2,1)}, u32[]{:S(2)}) copy-start(bf16[128,768]{1,0:T(8,128)(2,1)} %constant.19.clone.back) | copy-start | bytes 589828
  78.4 11.1 %copy-start.2 = (bf16[128,1024]{1,0:T(8,128)(2,1)S(1)}, bf16[128,1024]{1,0:T(8,128)(2,1)}, u32[]{:S(2)}) copy-start(bf16[128,1024]{1,0:T(8,128)(2,1)} %out_grad.1) | copy-start | bytes 786436
  78.4 11.1 %copy-start.5 = (bf16[128,1024]{1,0:T(8,128)(2,1)S(1)}, bf16[128,1024]{1,0:T(8,128)(2,1)}, u32[]{:S(2)}) copy-start(bf16[128,1024]{1,0:T(8,128)(2,1)} %copy-done.4) | copy-start | bytes 786436
  78.4 27.8 %all-to-all-start.2 = ((bf16[128,5,2,128]{3,2,1,0:T(2,128)(2,1)}), bf16[128,5,2,128]{3,2,1,0:T(2,128)(2,1)S(1)}, u32[]{:S(2)}, u32[]{:S(2)}) async-start(bf16[128,5,2,128]{3,2,1,0:T(2,128)(2,1)} %broadcast_in_dim.2), calls=%async_computation.2 | async-start | bytes 655360 | tf_op jit(solution)/shard_map/all_to_all | solution.py:223

commit v4 on v3

--- a/solution.py
+++ b/solution.py
@@ -65,11 +65,12 @@
     win[HALO:] = prod.astype(F32)
 
 
-def se_kernel(
-    key, value, query, rim, taps, grad, taps_mr, half, conv, mixed, square, kernel, near, win
-):
-    kernel[...] = to_spectrum(half[...], taps_mr[...])
+def spectra_kernel(grad, taps, half, kernel, near):
+    kernel[...] = to_spectrum(half[...], taps[...])
     near[...] = to_spectrum(half[...], grad[...])
+
+
+def se_kernel(key, value, query, rim, taps, conv, mixed, square, win):
     se_window(win, rim, key, value)
     f = taps[...].astype(F32)
     total = f[0:1] * win[HALO : HALO + 128]
@@ -172,8 +173,8 @@
     out_value[...] = (total * key_se[...].astype(F32)).astype(BF16)
 
 
-def gate_kernel(got, rim_mr, rim_se, out):
-    del got, rim_mr, rim_se, out
+def gate_kernel(total, rim_mr, rim_se, out):
+    del total, rim_mr, rim_se, out
 
 
 def wide(rows):
@@ -205,24 +206,27 @@
 
 def filter_totals(tiles, small, rims):
     n = lax.axis_size("ctx")
+    plane = n // 2
+    planes = [list(range(plane)), list(range(plane, n))]
     cols = small.shape[1]
-    rows = small.reshape(8, -1, 128).transpose(1, 0, 2).reshape(-1, 1, 1, 128).astype(BF16)
-    rows = jnp.pad(rows, ((0, n - rows.shape[0]), (0, 0), (0, 1), (0, 0)))
-    packed = jnp.concatenate([tiles.reshape(n, 4, 2, 128), rows], axis=1)
-    got = lax.all_to_all(packed, "ctx", 0, 0, tiled=True)
+    rows = small.reshape(8, -1, 128).transpose(1, 0, 2).reshape(plane, 1, 1, 128).astype(BF16)
+    rows = jnp.pad(rows, ((0, 0), (0, 0), (0, 1), (0, 0)))
+    packed = jnp.concatenate([tiles.reshape(plane, 8, 2, 128), rows], axis=1)
+    got = lax.all_to_all(packed, "ctx", 0, 0, axis_index_groups=planes, tiled=True)
+    part = jnp.sum(got.astype(F32), axis=0)
+    total = part + lax.ppermute(part, "ctx", [(i, (i + plane) % n) for i in range(n)])
     anywhere = pl.BlockSpec(memory_space=pl.ANY)
-    got = pl.pallas_call(
+    total = pl.pallas_call(
         gate_kernel,
         in_specs=[anywhere] * 3,
         out_specs=anywhere,
-        out_shape=jax.ShapeDtypeStruct(got.shape, BF16),
+        out_shape=jax.ShapeDtypeStruct(total.shape, F32),
         input_output_aliases={0: 0},
-    )(got, *rims)
-    total = lax.optimization_barrier(jnp.sum(got.astype(F32), axis=0)).astype(BF16)
-    spread = jnp.broadcast_to(total[None], (n,) + total.shape)
-    back = lax.all_to_all(spread, "ctx", 0, 0, tiled=True)
-    mr_sum = back[:, :4].reshape(tiles.shape).astype(F32).transpose(0, 2, 1, 3).reshape(-1, cols)
-    small_sum = back[: cols // 16, 4, 0].astype(F32).reshape(-1, 8, 128)
+    )(total, *rims)
+    spread = jnp.broadcast_to(total.astype(BF16)[None], (plane,) + total.shape)
+    back = lax.all_to_all(spread, "ctx", 0, 0, axis_index_groups=planes, tiled=True)
+    mr_sum = back[:, :8].reshape(tiles.shape).astype(F32).transpose(0, 2, 1, 3).reshape(-1, cols)
+    small_sum = back[:, 8, 0].astype(F32).reshape(-1, 8, 128)
     return mr_sum, small_sum.transpose(1, 0, 2).reshape(8, cols)
 
 
@@ -240,16 +244,26 @@
     rim_grad_mr = shifted(grad_conv_mr, "ctx", -1)
     half_spec, back_spec = fixed(*half.shape), fixed(*back_first.shape)
     spectral = (2 * tokens, cols)
-    conv_se, mixed_se, square, kernel_mr, near = call(
+    kernel_mr, near = call(
+        spectra_kernel,
+        cols,
+        [wide(tokens)] * 2 + [half_spec],
+        [wide(2 * tokens)] * 2,
+        [(spectral, F32)] * 2,
+        [],
+        2000 * tokens * cols,
+        20 * tokens * cols,
+    )(grad_conv_mr, filter_mr, half)
+    conv_se, mixed_se, square = call(
         se_kernel,
         cols,
-        [wide(tokens)] * 3 + [wide(HALO), wide(se_taps)] + [wide(tokens)] * 2 + [half_spec],
-        [wide(tokens), wide(tokens), fixed(tokens, 128)] + [wide(2 * tokens)] * 2,
-        [(full, F32), (full, F32), ((tokens, 128), F32), (spectral, F32), (spectral, F32)],
+        [wide(tokens)] * 3 + [wide(HALO), wide(se_taps)],
+        [wide(tokens), wide(tokens), fixed(tokens, 128)],
+        [(full, F32), (full, F32), ((tokens, 128), F32)],
         [pltpu.VMEM((tokens + HALO, WIDTH), F32)],
-        2000 * tokens * cols,
+        18 * tokens * cols,
         14 * tokens * cols,
-    )(key_se, value_path, query_se, rim_se, filter_se, grad_conv_mr, filter_mr, half)
+    )(key_se, value_path, query_se, rim_se, filter_se)
     grad_prod_mr, spectrum, stats = call(
         dot_kernel,
         cols,

time: 109 us -> 100 us (0.917)
  waiting for transfers between devices: 29.5 us -> 24.1 us
  starting transfers between devices: 51.3 us -> 47.5 us
    ppermute x4, waiting for transfers between devices: 11.1 us -> 2.42 us  [shifted(): return lax.ppermute(block, axis, route)]
    all_to_all x2, starting transfers between devices: 28.4 us -> 20.4 us  [the longest x1 14.2 us: filter_totals(): lax.all_to_all(packed, 'ctx', 0, 0, axis_index_groups=planes, tiled=True)]
    ppermute x0 -> x1, starting transfers between devices: none -> 4.28 us  [filter_totals(): lax.ppermute(part, 'ctx', [(i, (i + plane) % n) for i in range(n)])]
    ppermute x0 -> x1, waiting for transfers between devices: none -> 1.63 us  [filter_totals(): lax.ppermute(part, 'ctx', [(i, (i + plane) % n) for i in range(n)])]
    all_to_all x2, waiting for transfers between devices: 18.4 us -> 20 us  [the longest x1 11 us: filter_totals(): lax.all_to_all(spread, 'ctx', 0, 0, axis_index_groups=planes, tiled=True)]
    unnamed x38 -> x34, local copies, waits for them, and re-layouts: 2.66 us -> 2.32 us
  transfers between devices with their start and end apart: 6 -> 7, of which waited for: 5 -> 4; matrix products, arithmetic and copies ran while one was open for 0% -> 1% of each run, Pallas kernels for 3% -> 4%
where the time goes in v4:
time: 100 us; the launch traced here: 99.9 us
  starting transfers between devices  47.5 us (48%)
  waiting for transfers between devices  24.1 us (24%)
  blocking collectives  11.4 us (11%)
  Pallas kernels  6.68 us (7%)
  local copies, waits for them, and re-layouts  4.65 us (5%)
  other arithmetic  4.63 us (5%)
    ppermute x4, starting transfers between devices, shifted(): return lax.ppermute(block, axis, route)  22.9 us
    all_to_all x1, starting transfers between devices, filter_totals(): lax.all_to_all(packed, 'ctx', 0, 0, axis_index_groups=planes, tiled=True)  14.2 us
    all_to_all x1, blocking collectives, shards(): stats = lax.all_to_all(stats, 'tp', 0, 0, tiled=True)  11.4 us
    all_to_all x1, waiting for transfers between devices, filter_totals(): lax.all_to_all(spread, 'ctx', 0, 0, axis_index_groups=planes, tiled=True)  11 us
    all_to_all x1, waiting for transfers between devices, filter_totals(): lax.all_to_all(packed, 'ctx', 0, 0, axis_index_groups=planes, tiled=True)  9.03 us
    all_to_all x1, starting transfers between devices, filter_totals(): lax.all_to_all(spread, 'ctx', 0, 0, axis_index_groups=planes, tiled=True)  6.16 us
    ppermute x1, starting transfers between devices, filter_totals(): lax.ppermute(part, 'ctx', [(i, (i + plane) % n) for i in range(n)])  4.28 us
    ppermute x4, waiting for transfers between devices, shifted(): return lax.ppermute(block, axis, route)  2.42 us
  transfers between devices with their start and end apart: 7, of which 4 were waited for; matrix products, arithmetic and copies ran while one was open for 1% of the time, Pallas kernels for 4%

profile of v4, /device:TPU:2, one launch (start us, length us, event | category | flops | bytes accessed | tf_op | source)
XLA Modules:
  0.0 99.9 jit_solution(6304565799894753092)
XLA Ops:
  0.6 0.0 copy-start.12
  0.6 0.0 copy-start
  0.7 0.0 copy-start.1
  0.7 1.2 %multiply_convert_fusion.grad = bf16[128,1024]{1,0:T(8,128)(2,1)S(1)} fusion(bf16[128,1024]{1,0:T(8,128)(2,1)} %param.18, bf16[128,1024]{1,0:T(8,128)(2,1)} %out_grad.1), kind=kLoop, calls=%fused_computation.3 | loop fusion | flops 524288 | bytes 786432 | tf_op jit(solution)/shard_map/convert_element_type | solution.py:242
  1.8 0.0 copy-start.16
  1.8 15.1 %collective-permute-start = (bf16[128,1024]{1,0:T(8,128)(2,1)S(1)}, bf16[128,1024]{1,0:T(8,128)(2,1)S(1)}, u32[]{:S(2)}, u32[]{:S(2)}) collective-permute-start(bf16[128,1024]{1,0:T(8,128)(2,1)S(1)} %multiply_convert_fusion.grad), channel_id=1, source_target_pairs={{8,0},{16,8},{24,16},{32,24},{40,32},{48,40},{56,48},{64,56},{72,6... | collective-permute-start | bytes 786440 | tf_op jit(solution)/shard_map/ppermute | solution.py:204
  16.9 0.0 copy-done
  17.0 0.0 copy-done.1
  17.0 1.9 %collective-permute-start.1 = (bf16[16,1024]{1,0:T(8,128)(2,1)S(1)}, bf16[16,1024]{1,0:T(8,128)(2,1)S(1)}, u32[]{:S(2)}, u32[]{:S(2)}) collective-permute-start(bf16[16,1024]{1,0:T(8,128)(2,1)S(1)} %multiply_convert_fusion.1), channel_id=1, source_target_pairs={{0,8},{8,16},{16,24},{24,32},{32,40},{40,48},{48,56},{56,64},{64,7... | collective-permute-start | bytes 98312 | tf_op jit(solution)/shard_map/ppermute | solution.py:204
  18.9 0.0 copy-done.16
  18.9 0.0 copy-done.12
  18.9 0.0 copy-start.15
  19.0 0.9 copy-done.15
  19.9 0.0 copy-start.2
  19.9 0.0 copy-start.14
  19.9 0.4 shard_map.197
  20.3 0.0 copy-start.6
  20.4 0.0 copy-start.7
  20.4 0.0 copy-start.13
  20.4 2.4 %collective-permute-done.1.rim = bf16[16,1024]{1,0:T(8,128)(2,1)S(1)} collective-permute-done((bf16[16,1024]{1,0:T(8,128)(2,1)S(1)}, bf16[16,1024]{1,0:T(8,128)(2,1)S(1)}, u32[]{:S(2)}, u32[]{:S(2)}) %collective-permute-start.1) | collective-permute-done | bytes 32800 | tf_op jit(solution)/shard_map/ppermute | solution.py:204
  22.8 0.0 copy-done.2
  22.8 0.0 copy-done.14
  22.8 1.0 %shard_map.198 = (f32[128,1024]{1,0:T(8,128)S(1)}, f32[128,1024]{1,0:T(8,128)S(1)}, f32[128,128]{1,0:T(8,128)S(1)}) custom-call(bf16[128,1024]{1,0:T(8,128)(2,1)S(1)} %copy-done, bf16[128,1024]{1,0:T(8,128)(2,1)S(1)} %copy-done.1, bf16[128,1024]{1,0:T(8,128)(2,1)S(1)} %copy-done.2, bf16[16,1024]{1,0:T(8,128)(2,1)S(1)} %collective-permute-done.1.rim, ...), custom_call_target="tpu_custom_call" | custom-call | flops 2359296 | bytes 1835008 | tf_op jit(solution)/shard_map/pallas_call | solution.py:257
  23.8 0.0 collective-permute-done.rim
  23.8 0.0 copy-done.6
  23.8 0.0 copy-done.7
  23.8 0.0 copy-done.13
  23.9 0.9 shard_map.199
  24.8 11.4 %all_to_all.15.stats = f32[8,8,128]{2,1,0:T(8,128)S(1)} all-to-all(f32[8,8,128]{2,1,0:T(8,128)S(1)} %get-tuple-element.30), channel_id=1, replica_groups=mesh['ctx'=128,'tp'=8] {'tp'}, dimensions={0} | all-to-all | bytes 65536 | tf_op jit(solution)/shard_map/all_to_all | solution.py:278
  36.2 1.9 %shard_map.200 = (bf16[128,1024]{1,0:T(8,128)(2,1)}, bf16[128,1024]{1,0:T(8,128)(2,1)}, bf16[128,1024]{1,0:T(8,128)(2,1)S(1)}, bf16[128,1024]{1,0:T(8,128)(2,1)S...) custom-call(f32[8,8,128]{2,1,0:T(8,128)S(1)} %all_to_all.15.stats, ...), custom_call_target="tpu_custom_call" | custom-call | flops 262144000 | bytes 5242880 | tf_op jit(solution)/shard_map/pallas_call | solution.py:282
  38.2 1.0 fusion
  39.2 14.2 %all-to-all-start.1 = ((bf16[64,9,2,128]{3,2,1,0:T(2,128)(2,1)}), bf16[64,9,2,128]{3,2,1,0:T(2,128)(2,1)S(1)}, u32[]{:S(2)}, u32[]{:S(2)}) async-start(bf16[64,9,2,128]{3,2,1,0:T(2,128)(2,1)} %fusion), calls=%async_computation.1 | async-start | bytes 589824 | tf_op jit(solution)/shard_map/all_to_all | solution.py:215
  53.4 3.4 %collective-permute-start.2 = (bf16[128,1024]{1,0:T(8,128)(2,1)S(1)}, bf16[128,1024]{1,0:T(8,128)(2,1)S(1)}, u32[]{:S(2)}, u32[]{:S(2)}) collective-permute-start(bf16[128,1024]{1,0:T(8,128)(2,1)S(1)} %get-tuple-element.34.prod_mr), channel_id=1, source_target_pairs={{0,8},{8,16},{16,24},{24,32},{32,40},{40,48},{48,56},{56,64},{64,7... | collective-permute-start | bytes 786440 | tf_op jit(solution)/shard_map/ppermute | solution.py:204
  56.8 2.5 %collective-permute-start.3 = (bf16[16,1024]{1,0:T(8,128)(2,1)S(1)}, bf16[16,1024]{1,0:T(8,128)(2,1)S(1)}, u32[]{:S(2)}, u32[]{:S(2)}) collective-permute-start(bf16[16,1024]{1,0:T(8,128)(2,1)S(1)} %get-tuple-element.36), channel_id=1, source_target_pairs={{8,0},{16,8},{24,16},{32,24},{40,32},{48,40},{56,48},{64,56},{72,6... | collective-permute-start | bytes 98312 | tf_op jit(solution)/shard_map/ppermute | solution.py:204
  59.3 9.0 %all-to-all-done.1 = bf16[64,9,2,128]{3,2,1,0:T(2,128)(2,1)S(1)} async-done(((bf16[64,9,2,128]{3,2,1,0:T(2,128)(2,1)}), bf16[64,9,2,128]{3,2,1,0:T(2,128)(2,1)S(1)}, u32[]{:S(2)}, u32[]{:S(2)}) %all-to-all-start.1) | async-done | bytes 294944 | tf_op jit(solution)/shard_map/all_to_all | solution.py:215
  68.3 0.3 convert_reduce_fusion
  68.6 4.3 %collective-permute-start.4 = (f32[9,2,128]{2,1,0:T(2,128)S(1)}, f32[9,2,128]{2,1,0:T(2,128)S(1)}, u32[]{:S(2)}, u32[]{:S(2)}) collective-permute-start(f32[9,2,128]{2,1,0:T(2,128)S(1)} %convert_reduce_fusion), channel_id=1, source_target_pairs={{0,512},{8,520},{16,528},{24,536},{32,544},{40,552},{48,560},{56,5... | collective-permute-start | bytes 27656 | tf_op jit(solution)/shard_map/ppermute | solution.py:217
  72.8 1.6 %collective-permute-done.4 = f32[9,2,128]{2,1,0:T(2,128)S(1)} collective-permute-done((f32[9,2,128]{2,1,0:T(2,128)S(1)}, f32[9,2,128]{2,1,0:T(2,128)S(1)}, u32[]{:S(2)}, u32[]{:S(2)}) %collective-permute-start.4) | collective-permute-done | bytes 9248 | tf_op jit(solution)/shard_map/ppermute | solution.py:217
  74.5 0.6 add.5.total
  75.1 0.0 collective-permute-done.3.rim_se
  75.1 0.0 copy-start.10
  75.1 0.0 collective-permute-done.2.rim_mr
  75.1 0.6 copy-done.10
  75.7 0.0 copy-start.4
  75.7 0.7 copy-done.4
  76.4 0.0 copy-start.9
  76.4 0.7 convert_element_type.66
  77.1 0.0 copy-start.8
  77.1 0.9 broadcast_in_dim.2
  78.0 0.0 copy-start.3
  78.0 0.0 copy-start.5
  78.0 0.0 copy-start.11
  78.0 6.2 %all-to-all-start.2 = ((bf16[64,9,2,128]{3,2,1,0:T(2,128)(2,1)}), bf16[64,9,2,128]{3,2,1,0:T(2,128)(2,1)S(1)}, u32[]{:S(2)}, u32[]{:S(2)}) async-start(bf16[64,9,2,128]{3,2,1,0:T(2,128)(2,1)} %broadcast_in_dim.2), calls=%async_computation.2 | async-start | bytes 589824 | tf_op jit(solution)/shard_map/all_to_all | solution.py:227
  84.2 0.0 copy-done.9
  84.2 0.0 copy-done.8
  84.2 0.0 copy-done.3
  84.2 0.0 copy-done.5
  84.2 0.0 copy-done.11
  84.2 2.4 %shard_map.201 = (bf16[128,1024]{1,0:T(8,128)(2,1)}, bf16[128,1024]{1,0:T(8,128)(2,1)}, bf16[128,1024]{1,0:T(8,128)(2,1)}) custom-call(bf16[128,1024]{1,0:T(8,128)(2,1)S(1)} %get-tuple-element.34.prod_mr, bf16[128,1024]{1,0:T(8,128)(2,1)S(1)} %copy-done.5, bf16[128,1024]{1,0:T(8,128)(2,1)S(1)} %copy-done.3, f32[256,1024]{1,0:T(8,128)S(1)} %get-tuple-element.27.kernel, ...), custom_call_target="tpu_custom_call" | custom-call | flops 393216000 | bytes 2621440 | tf_op jit(solution)/shard_map/pallas_call | solution.py:302
  86.6 11.0 %all-to-all-done.2 = bf16[64,9,2,128]{3,2,1,0:T(2,128)(2,1)S(1)} async-done(((bf16[64,9,2,128]{3,2,1,0:T(2,128)(2,1)}), bf16[64,9,2,128]{3,2,1,0:T(2,128)(2,1)S(1)}, u32[]{:S(2)}, u32[]{:S(2)}) %all-to-all-start.2) | async-done | bytes 294944 | tf_op jit(solution)/shard_map/all_to_all | solution.py:227
  97.6 0.6 slice.32
  98.2 0.6 slice_bitcast_fusion
  98.9 0.2 slice.31
  99.1 0.8 convert_bitcast_fusion
  (7 shorter events, 0.1 us)
Async XLA Ops:
  0.6 18.3 %copy-start.12 = (bf16[256,256]{1,0:T(8,128)(2,1)S(1)}, bf16[256,256]{1,0:T(8,128)(2,1)}, u32[]{:S(2)}) copy-start(bf16[256,256]{1,0:T(8,128)(2,1)} %constant.16.clone.half) | copy-start | bytes 393220
  0.6 16.3 %copy-start = (bf16[128,1024]{1,0:T(8,128)(2,1)S(1)}, bf16[128,1024]{1,0:T(8,128)(2,1)}, u32[]{:S(2)}) copy-start(bf16[128,1024]{1,0:T(8,128)(2,1)} %key_se.3) | copy-start | bytes 786436
  0.7 16.3 %copy-start.1 = (bf16[128,1024]{1,0:T(8,128)(2,1)S(1)}, bf16[128,1024]{1,0:T(8,128)(2,1)}, u32[]{:S(2)}) copy-start(bf16[128,1024]{1,0:T(8,128)(2,1)} %value.5) | copy-start | bytes 786436
  1.8 17.1 %copy-start.16 = (bf16[1024]{0:T(1024)(128)(2,1)S(1)}, bf16[1024]{0:T(1024)(128)(2,1)}, u32[]{:S(2)}) copy-start(bf16[1024]{0:T(1024)(128)(2,1)} %param.20) | copy-start | bytes 6148
  1.8 22.0 %collective-permute-start = (bf16[128,1024]{1,0:T(8,128)(2,1)S(1)}, bf16[128,1024]{1,0:T(8,128)(2,1)S(1)}, u32[]{:S(2)}, u32[]{:S(2)}) collective-permute-start(bf16[128,1024]{1,0:T(8,128)(2,1)S(1)} %multiply_convert_fusion.grad), channel_id=1, source_target_pairs={{8,0},{16,8},{24,16},{32,24},{40,32},{48,40},{56,48},{64,56},{72,6... | collective-permute-start | bytes 786440 | tf_op jit(solution)/shard_map/ppermute | solution.py:204
  17.0 5.8 %collective-permute-start.1 = (bf16[16,1024]{1,0:T(8,128)(2,1)S(1)}, bf16[16,1024]{1,0:T(8,128)(2,1)S(1)}, u32[]{:S(2)}, u32[]{:S(2)}) collective-permute-start(bf16[16,1024]{1,0:T(8,128)(2,1)S(1)} %multiply_convert_fusion.1), channel_id=1, source_target_pairs={{0,8},{8,16},{16,24},{24,32},{32,40},{40,48},{48,56},{56,64},{64,7... | collective-permute-start | bytes 98312 | tf_op jit(solution)/shard_map/ppermute | solution.py:204
  18.9 1.0 copy-start.15
  19.9 2.9 %copy-start.2 = (bf16[128,1024]{1,0:T(8,128)(2,1)S(1)}, bf16[128,1024]{1,0:T(8,128)(2,1)}, u32[]{:S(2)}) copy-start(bf16[128,1024]{1,0:T(8,128)(2,1)} %query_se.1) | copy-start | bytes 786436
  19.9 2.9 %copy-start.14 = (bf16[7,1024]{1,0:T(8,128)(2,1)S(1)}, bf16[7,1024]{1,0:T(8,128)(2,1)}, u32[]{:S(2)}) copy-start(bf16[7,1024]{1,0:T(8,128)(2,1)} %taps_se.1) | copy-start | bytes 43012
  20.3 3.5 %copy-start.6 = (bf16[128,1024]{1,0:T(8,128)(2,1)S(1)}, bf16[128,1024]{1,0:T(8,128)(2,1)}, u32[]{:S(2)}) copy-start(bf16[128,1024]{1,0:T(8,128)(2,1)} %key_mr.1) | copy-start | bytes 786436
  20.4 3.5 %copy-start.7 = (bf16[128,768]{1,0:T(8,128)(2,1)S(1)}, bf16[128,768]{1,0:T(8,128)(2,1)}, u32[]{:S(2)}) copy-start(bf16[128,768]{1,0:T(8,128)(2,1)} %constant.18.clone.back) | copy-start | bytes 589828
  20.4 3.5 %copy-start.13 = (bf16[256,256]{1,0:T(8,128)(2,1)S(1)}, bf16[256,256]{1,0:T(8,128)(2,1)}, u32[]{:S(2)}) copy-start(bf16[256,256]{1,0:T(8,128)(2,1)} %constant.17.clone.later) | copy-start | bytes 393220
  39.2 29.1 %all-to-all-start.1 = ((bf16[64,9,2,128]{3,2,1,0:T(2,128)(2,1)}), bf16[64,9,2,128]{3,2,1,0:T(2,128)(2,1)S(1)}, u32[]{:S(2)}, u32[]{:S(2)}) async-start(bf16[64,9,2,128]{3,2,1,0:T(2,128)(2,1)} %fusion), calls=%async_computation.1 | async-start | bytes 589824 | tf_op jit(solution)/shard_map/all_to_all | solution.py:215
  53.4 21.7 %collective-permute-start.2 = (bf16[128,1024]{1,0:T(8,128)(2,1)S(1)}, bf16[128,1024]{1,0:T(8,128)(2,1)S(1)}, u32[]{:S(2)}, u32[]{:S(2)}) collective-permute-start(bf16[128,1024]{1,0:T(8,128)(2,1)S(1)} %get-tuple-element.34.prod_mr), channel_id=1, source_target_pairs={{0,8},{8,16},{16,24},{24,32},{32,40},{40,48},{48,56},{56,64},{64,7... | collective-permute-start | bytes 786440 | tf_op jit(solution)/shard_map/ppermute | solution.py:204
  56.8 18.3 %collective-permute-start.3 = (bf16[16,1024]{1,0:T(8,128)(2,1)S(1)}, bf16[16,1024]{1,0:T(8,128)(2,1)S(1)}, u32[]{:S(2)}, u32[]{:S(2)}) collective-permute-start(bf16[16,1024]{1,0:T(8,128)(2,1)S(1)} %get-tuple-element.36), channel_id=1, source_target_pairs={{8,0},{16,8},{24,16},{32,24},{40,32},{48,40},{56,48},{64,56},{72,6... | collective-permute-start | bytes 98312 | tf_op jit(solution)/shard_map/ppermute | solution.py:204
  68.6 5.9 %collective-permute-start.4 = (f32[9,2,128]{2,1,0:T(2,128)S(1)}, f32[9,2,128]{2,1,0:T(2,128)S(1)}, u32[]{:S(2)}, u32[]{:S(2)}) collective-permute-start(f32[9,2,128]{2,1,0:T(2,128)S(1)} %convert_reduce_fusion), channel_id=1, source_target_pairs={{0,512},{8,520},{16,528},{24,536},{32,544},{40,552},{48,560},{56,5... | collective-permute-start | bytes 27656 | tf_op jit(solution)/shard_map/ppermute | solution.py:217
  75.1 0.6 copy-start.10
  75.7 0.7 copy-start.4
  76.4 7.8 %copy-start.9 = (bf16[128,768]{1,0:T(8,128)(2,1)S(1)}, bf16[128,768]{1,0:T(8,128)(2,1)}, u32[]{:S(2)}) copy-start(bf16[128,768]{1,0:T(8,128)(2,1)} %constant.19.clone.back) | copy-start | bytes 589828
  77.1 7.1 %copy-start.8 = (bf16[256,512]{1,0:T(8,128)(2,1)S(1)}, bf16[256,512]{1,0:T(8,128)(2,1)}, u32[]{:S(2)}) copy-start(bf16[256,512]{1,0:T(8,128)(2,1)} %constant.15.clone.whole) | copy-start | bytes 786436
  78.0 6.2 %copy-start.3 = (bf16[128,1024]{1,0:T(8,128)(2,1)S(1)}, bf16[128,1024]{1,0:T(8,128)(2,1)}, u32[]{:S(2)}) copy-start(bf16[128,1024]{1,0:T(8,128)(2,1)} %out_grad.1) | copy-start | bytes 786436
  78.0 6.2 %copy-start.5 = (bf16[128,1024]{1,0:T(8,128)(2,1)S(1)}, bf16[128,1024]{1,0:T(8,128)(2,1)}, u32[]{:S(2)}) copy-start(bf16[128,1024]{1,0:T(8,128)(2,1)} %copy-done.4) | copy-start | bytes 786436
  78.0 6.2 %copy-start.11 = (bf16[16,1024]{1,0:T(8,128)(2,1)S(1)}, bf16[16,1024]{1,0:T(8,128)(2,1)}, u32[]{:S(2)}) copy-start(bf16[16,1024]{1,0:T(8,128)(2,1)} %copy-done.10) | copy-start | bytes 98308
  78.0 19.6 %all-to-all-start.2 = ((bf16[64,9,2,128]{3,2,1,0:T(2,128)(2,1)}), bf16[64,9,2,128]{3,2,1,0:T(2,128)(2,1)S(1)}, u32[]{:S(2)}, u32[]{:S(2)}) async-start(bf16[64,9,2,128]{3,2,1,0:T(2,128)(2,1)} %broadcast_in_dim.2), calls=%async_computation.2 | async-start | bytes 589824 | tf_op jit(solution)/shard_map/all_to_all | solution.py:227

commit v5 on v4

--- a/solution.py
+++ b/solution.py
@@ -173,8 +173,18 @@
     out_value[...] = (total * key_se[...].astype(F32)).astype(BF16)
 
 
-def gate_kernel(total, rim_mr, rim_se, out):
-    del total, rim_mr, rim_se, out
+def plane_kernel(part, other, rim_mr, rim_se, out):
+    del rim_mr, rim_se
+    out[...] = (part[...] + other[...]).astype(BF16)
+
+
+def unpack_kernel(tiles, small, out_mr, out_se, out_gain):
+    taps = out_se.shape[0]
+    for b in range(small.shape[0]):
+        lanes = slice(128 * b, 128 * b + 128)
+        out_mr[:, lanes] = tiles[:, b].astype(F32).reshape(out_mr.shape[0], 128)
+        out_se[:, lanes] = small[b, :taps]
+        out_gain[:, lanes] = small[b, taps:]
 
 
 def wide(rows):
@@ -214,20 +224,18 @@
     packed = jnp.concatenate([tiles.reshape(plane, 8, 2, 128), rows], axis=1)
     got = lax.all_to_all(packed, "ctx", 0, 0, axis_index_groups=planes, tiled=True)
     part = jnp.sum(got.astype(F32), axis=0)
-    total = part + lax.ppermute(part, "ctx", [(i, (i + plane) % n) for i in range(n)])
-    anywhere = pl.BlockSpec(memory_space=pl.ANY)
+    other = lax.ppermute(part, "ctx", [(i, (i + plane) % n) for i in range(n)])
     total = pl.pallas_call(
-        gate_kernel,
-        in_specs=[anywhere] * 3,
-        out_specs=anywhere,
-        out_shape=jax.ShapeDtypeStruct(total.shape, F32),
-        input_output_aliases={0: 0},
-    )(total, *rims)
-    spread = jnp.broadcast_to(total.astype(BF16)[None], (plane,) + total.shape)
+        plane_kernel,
+        out_shape=jax.ShapeDtypeStruct(part.shape, BF16),
+    )(part, other, *[rim[:HALO, :128] for rim in rims])
+    spread = jnp.broadcast_to(total[None], (plane,) + total.shape)
     back = lax.all_to_all(spread, "ctx", 0, 0, axis_index_groups=planes, tiled=True)
-    mr_sum = back[:, :8].reshape(tiles.shape).astype(F32).transpose(0, 2, 1, 3).reshape(-1, cols)
-    small_sum = back[:, 8, 0].astype(F32).reshape(-1, 8, 128)
-    return mr_sum, small_sum.transpose(1, 0, 2).reshape(8, cols)
+    mr_shape, se_shape = (tiles.shape[0] * 8, cols), (small.shape[0] - 1, cols)
+    return pl.pallas_call(
+        unpack_kernel,
+        out_shape=[jax.ShapeDtypeStruct(shape, F32) for shape in (mr_shape, se_shape, (1, cols))],
+    )(back[:, :8].reshape(tiles.shape), back[:, 8, 0].astype(F32).reshape(-1, 8, 128))
 
 
 def shards(
@@ -298,7 +306,7 @@
     )
     rim_mr = shifted(prod_mr, "ctx", 1)
     rim_grad_se = shifted(head, "ctx", -1)
-    grad_filter_mr, small = filter_totals(tiles, small, (rim_mr, rim_grad_se))
+    grad_filter_mr, grad_filter_se, grad_gain = filter_totals(tiles, small, (rim_mr, rim_grad_se))
     grad_query_mr, grad_key_se, grad_value = call(
         last_kernel,
         cols,
@@ -319,9 +327,9 @@
         grad_key_se,
         grad_query_mr,
         grad_key_mr,
-        small[:se_taps],
+        grad_filter_se,
         grad_filter_mr,
-        small[se_taps],
+        grad_gain.reshape(cols),
     )
 
 

time: 100 us -> 101 us (1.010)
  Pallas kernels: 6.68 us -> 9.72 us
  other arithmetic: 4.63 us -> 3.05 us
  waiting for transfers between devices: 24.1 us -> 22.9 us
    pallas_call x1 -> x2, Pallas kernels: 0.01 us -> 3.13 us  [the longest x1 1.8 us: filter_totals(): pl.pallas_call(unpack_kernel, out_shape=[jax.ShapeDtypeStruct(shape, F32)...]
    ppermute x1, waiting for transfers between devices: 1.63 us -> 0.42 us  [filter_totals(): other = lax.ppermute(part, 'ctx', [(i, (i + plane) % n) for i in range(n)])]
    unnamed x34 -> x30, local copies, waits for them, and re-layouts: 2.32 us -> 1.61 us
    slice x4 -> x3, local copies, waits for them, and re-layouts: 1.42 us -> 2.07 us  [the longest x2 1.19 us: filter_totals(): rim[:HALO, :128]]
where the time goes in v5:
time: 101 us
  starting transfers between devices  47.5 us (47%)
  waiting for transfers between devices  22.9 us (23%)
  blocking collectives  11.4 us (11%)
  Pallas kernels  9.72 us (10%)
  local copies, waits for them, and re-layouts  5.3 us (5%)
  other arithmetic  3.05 us (3%)
    ppermute x4, starting transfers between devices, shifted(): return lax.ppermute(block, axis, route)  22.9 us
    all_to_all x1, starting transfers between devices, filter_totals(): lax.all_to_all(packed, 'ctx', 0, 0, axis_index_groups=planes, tiled=True)  14.2 us
    all_to_all x1, blocking collectives, shards(): stats = lax.all_to_all(stats, 'tp', 0, 0, tiled=True)  11.4 us
    all_to_all x1, waiting for transfers between devices, filter_totals(): lax.all_to_all(spread, 'ctx', 0, 0, axis_index_groups=planes, tiled=True)  11.1 us
    all_to_all x1, waiting for transfers between devices, filter_totals(): lax.all_to_all(packed, 'ctx', 0, 0, axis_index_groups=planes, tiled=True)  9.03 us
    all_to_all x1, starting transfers between devices, filter_totals(): lax.all_to_all(spread, 'ctx', 0, 0, axis_index_groups=planes, tiled=True)  6.16 us
    ppermute x1, starting transfers between devices, filter_totals(): other = lax.ppermute(part, 'ctx', [(i, (i + plane) % n) for i in range(n)])  4.29 us
    ppermute x4, waiting for transfers between devices, shifted(): return lax.ppermute(block, axis, route)  2.42 us
  transfers between devices with their start and end apart: 7, of which 4 were waited for; matrix products, arithmetic and copies ran while one was open for 1% of the time, Pallas kernels for 4%

profile of v5, /device:TPU:2, one launch (start us, length us, event | category | flops | bytes accessed | tf_op | source)
XLA Modules:
  0.0 100.9 jit_solution(14104125854981163903)
XLA Ops:
  0.6 0.0 copy-start.8
  0.6 0.0 copy-start
  0.7 0.0 copy-start.1
  0.7 1.2 %multiply_convert_fusion.grad = bf16[128,1024]{1,0:T(8,128)(2,1)S(1)} fusion(bf16[128,1024]{1,0:T(8,128)(2,1)} %param.18, bf16[128,1024]{1,0:T(8,128)(2,1)} %out_grad.1), kind=kLoop, calls=%fused_computation.2 | loop fusion | flops 524288 | bytes 786432 | tf_op jit(solution)/shard_map/convert_element_type | solution.py:250
  1.8 0.0 copy-start.14
  1.8 15.1 %collective-permute-start = (bf16[128,1024]{1,0:T(8,128)(2,1)S(1)}, bf16[128,1024]{1,0:T(8,128)(2,1)S(1)}, u32[]{:S(2)}, u32[]{:S(2)}) collective-permute-start(bf16[128,1024]{1,0:T(8,128)(2,1)S(1)} %multiply_convert_fusion.grad), channel_id=1, source_target_pairs={{8,0},{16,8},{24,16},{32,24},{40,32},{48,40},{56,48},{64,56},{72,6... | collective-permute-start | bytes 786440 | tf_op jit(solution)/shard_map/ppermute | solution.py:214
  16.9 0.0 copy-done
  17.0 0.0 copy-done.1
  17.0 1.9 %collective-permute-start.1 = (bf16[16,1024]{1,0:T(8,128)(2,1)S(1)}, bf16[16,1024]{1,0:T(8,128)(2,1)S(1)}, u32[]{:S(2)}, u32[]{:S(2)}) collective-permute-start(bf16[16,1024]{1,0:T(8,128)(2,1)S(1)} %multiply_convert_fusion.1), channel_id=1, source_target_pairs={{0,8},{8,16},{16,24},{24,32},{32,40},{40,48},{48,56},{56,64},{64,7... | collective-permute-start | bytes 98312 | tf_op jit(solution)/shard_map/ppermute | solution.py:214
  18.9 0.0 copy-done.14
  18.9 0.0 copy-done.8
  18.9 0.0 copy-start.11
  19.0 0.9 copy-done.11
  19.9 0.0 copy-start.2
  19.9 0.0 copy-start.10
  19.9 0.4 shard_map.197
  20.3 0.0 copy-start.4
  20.3 0.0 copy-start.5
  20.4 0.0 copy-start.9
  20.4 2.4 %collective-permute-done.1.rim = bf16[16,1024]{1,0:T(8,128)(2,1)S(1)} collective-permute-done((bf16[16,1024]{1,0:T(8,128)(2,1)S(1)}, bf16[16,1024]{1,0:T(8,128)(2,1)S(1)}, u32[]{:S(2)}, u32[]{:S(2)}) %collective-permute-start.1) | collective-permute-done | bytes 32800 | tf_op jit(solution)/shard_map/ppermute | solution.py:214
  22.8 0.0 copy-done.2
  22.8 0.0 copy-done.10
  22.8 1.0 %shard_map.198 = (f32[128,1024]{1,0:T(8,128)S(1)}, f32[128,1024]{1,0:T(8,128)S(1)}, f32[128,128]{1,0:T(8,128)S(1)}) custom-call(bf16[128,1024]{1,0:T(8,128)(2,1)S(1)} %copy-done, bf16[128,1024]{1,0:T(8,128)(2,1)S(1)} %copy-done.1, bf16[128,1024]{1,0:T(8,128)(2,1)S(1)} %copy-done.2, bf16[16,1024]{1,0:T(8,128)(2,1)S(1)} %collective-permute-done.1.rim, ...), custom_call_target="tpu_custom_call" | custom-call | flops 2359296 | bytes 1835008 | tf_op jit(solution)/shard_map/pallas_call | solution.py:265
  23.8 0.0 collective-permute-done.rim
  23.8 0.0 copy-done.4
  23.8 0.0 copy-done.5
  23.8 0.0 copy-done.9
  23.9 0.9 shard_map.199
  24.7 11.4 %all_to_all.15.stats = f32[8,8,128]{2,1,0:T(8,128)S(1)} all-to-all(f32[8,8,128]{2,1,0:T(8,128)S(1)} %get-tuple-element.33), channel_id=1, replica_groups=mesh['ctx'=128,'tp'=8] {'tp'}, dimensions={0} | all-to-all | bytes 65536 | tf_op jit(solution)/shard_map/all_to_all | solution.py:286
  36.2 1.9 %shard_map.200 = (bf16[128,1024]{1,0:T(8,128)(2,1)}, bf16[128,1024]{1,0:T(8,128)(2,1)}, bf16[128,1024]{1,0:T(8,128)(2,1)S(1)}, bf16[128,1024]{1,0:T(8,128)(2,1)S...) custom-call(f32[8,8,128]{2,1,0:T(8,128)S(1)} %all_to_all.15.stats, ...), custom_call_target="tpu_custom_call" | custom-call | flops 262144000 | bytes 5242880 | tf_op jit(solution)/shard_map/pallas_call | solution.py:290
  38.1 1.0 fusion
  39.1 14.2 %all-to-all-start.1 = ((bf16[64,9,2,128]{3,2,1,0:T(2,128)(2,1)}), bf16[64,9,2,128]{3,2,1,0:T(2,128)(2,1)S(1)}, u32[]{:S(2)}, u32[]{:S(2)}) async-start(bf16[64,9,2,128]{3,2,1,0:T(2,128)(2,1)} %fusion), calls=%async_computation.1 | async-start | bytes 589824 | tf_op jit(solution)/shard_map/all_to_all | solution.py:225
  53.3 3.4 %collective-permute-start.2 = (bf16[128,1024]{1,0:T(8,128)(2,1)S(1)}, bf16[128,1024]{1,0:T(8,128)(2,1)S(1)}, u32[]{:S(2)}, u32[]{:S(2)}) collective-permute-start(bf16[128,1024]{1,0:T(8,128)(2,1)S(1)} %get-tuple-element.37.prod_mr), channel_id=1, source_target_pairs={{0,8},{8,16},{16,24},{24,32},{32,40},{40,48},{48,56},{56,64},{64,7... | collective-permute-start | bytes 786440 | tf_op jit(solution)/shard_map/ppermute | solution.py:214
  56.7 2.5 %collective-permute-start.3 = (bf16[16,1024]{1,0:T(8,128)(2,1)S(1)}, bf16[16,1024]{1,0:T(8,128)(2,1)S(1)}, u32[]{:S(2)}, u32[]{:S(2)}) collective-permute-start(bf16[16,1024]{1,0:T(8,128)(2,1)S(1)} %get-tuple-element.39), channel_id=1, source_target_pairs={{8,0},{16,8},{24,16},{32,24},{40,32},{48,40},{56,48},{64,56},{72,6... | collective-permute-start | bytes 98312 | tf_op jit(solution)/shard_map/ppermute | solution.py:214
  59.2 9.0 %all-to-all-done.1 = bf16[64,9,2,128]{3,2,1,0:T(2,128)(2,1)S(1)} async-done(((bf16[64,9,2,128]{3,2,1,0:T(2,128)(2,1)}), bf16[64,9,2,128]{3,2,1,0:T(2,128)(2,1)S(1)}, u32[]{:S(2)}, u32[]{:S(2)}) %all-to-all-start.1) | async-done | bytes 294944 | tf_op jit(solution)/shard_map/all_to_all | solution.py:225
  68.2 0.3 convert_reduce_fusion.part
  68.5 0.0 copy-start.12
  68.5 4.3 %collective-permute-start.4 = (f32[9,2,128]{2,1,0:T(2,128)S(1)}, f32[9,2,128]{2,1,0:T(2,128)S(1)}, u32[]{:S(2)}, u32[]{:S(2)}) collective-permute-start(f32[9,2,128]{2,1,0:T(2,128)S(1)} %convert_reduce_fusion.part), channel_id=1, source_target_pairs={{0,512},{8,520},{16,528},{24,536},{32,544},{40,552},{48,560},{56,5... | collective-permute-start | bytes 27656 | tf_op jit(solution)/shard_map/ppermute | solution.py:227
  72.8 0.0 collective-permute-done.3.rim_se
  72.8 0.6 slice.25.rim_se
  73.4 0.0 collective-permute-done.2.rim_mr
  73.4 0.6 slice.24.rim_mr
  74.0 0.4 collective-permute-done.4.other
  74.4 0.0 copy-done.12
  74.4 0.0 copy-start.13
  74.4 0.6 copy-done.13
  75.0 1.3 %shard_map.202 = bf16[9,2,128]{2,1,0:T(2,128)(2,1)} custom-call(f32[9,2,128]{2,1,0:T(2,128)} %copy-done.12, f32[9,2,128]{2,1,0:T(2,128)} %copy-done.13, bf16[16,128]{1,0:T(8,128)(2,1)} %slice.24.rim_mr, bf16[16,128]{1,0:T(8,128)(2,1)} %slice.25.rim_se), custom_call_target="tpu_custom_call" | custom-call | tf_op jit(solution)/shard_map/pallas_call | solution.py:228
  76.3 0.0 copy-start.7
  76.3 1.6 %broadcast_in_dim.2 = bf16[64,9,2,128]{3,2,1,0:T(2,128)(2,1)} broadcast(bf16[9,2,128]{2,1,0:T(2,128)(2,1)} %shard_map.202), dimensions={1,2,3} | broadcast | bytes 299520 | tf_op jit(solution)/shard_map/broadcast_in_dim | solution.py:232
  77.9 0.0 copy-start.3
  77.9 0.0 copy-start.6
  77.9 6.2 %all-to-all-start.2 = ((bf16[64,9,2,128]{3,2,1,0:T(2,128)(2,1)}), bf16[64,9,2,128]{3,2,1,0:T(2,128)(2,1)S(1)}, u32[]{:S(2)}, u32[]{:S(2)}) async-start(bf16[64,9,2,128]{3,2,1,0:T(2,128)(2,1)} %broadcast_in_dim.2), calls=%async_computation.2 | async-start | bytes 589824 | tf_op jit(solution)/shard_map/all_to_all | solution.py:233
  84.1 0.0 copy-done.7
  84.1 0.0 copy-done.3
  84.1 0.0 copy-done.6
  84.1 2.4 %shard_map.201 = (bf16[128,1024]{1,0:T(8,128)(2,1)}, bf16[128,1024]{1,0:T(8,128)(2,1)}, bf16[128,1024]{1,0:T(8,128)(2,1)}) custom-call(bf16[128,1024]{1,0:T(8,128)(2,1)S(1)} %get-tuple-element.37.prod_mr, bf16[128,1024]{1,0:T(8,128)(2,1)S(1)} %collective-permute-done.2.rim_mr, bf16[128,1024]{1,0:T(8,128)(2,1)S(1)} %copy-done.3, ...), custom_call_target="tpu_custom_call" | custom-call | flops 393216000 | bytes 2621440 | tf_op jit(solution)/shard_map/pallas_call | solution.py:310
  86.5 11.1 %all-to-all-done.2 = bf16[64,9,2,128]{3,2,1,0:T(2,128)(2,1)S(1)} async-done(((bf16[64,9,2,128]{3,2,1,0:T(2,128)(2,1)}), bf16[64,9,2,128]{3,2,1,0:T(2,128)(2,1)S(1)}, u32[]{:S(2)}, u32[]{:S(2)}) %all-to-all-start.2) | async-done | bytes 294944 | tf_op jit(solution)/shard_map/all_to_all | solution.py:233
  97.6 0.6 slice_convert_fusion
  98.2 0.9 slice.26
  99.1 1.8 %shard_map.203 = (f32[128,1024]{1,0:T(8,128)}, f32[7,1024]{1,0:T(8,128)}, f32[1,1024]{1,0:T(1,128)}) custom-call(bf16[16,8,8,128]{3,2,1,0:T(8,128)(2,1)} %bitcast.11, f32[8,8,128]{2,1,0:T(8,128)} %bitcast.12), custom_call_target="tpu_custom_call" | custom-call | tf_op jit(solution)/shard_map/pallas_call | solution.py:235
  (4 shorter events, 0.1 us)
Async XLA Ops:
  0.6 18.3 %copy-start.8 = (bf16[256,256]{1,0:T(8,128)(2,1)S(1)}, bf16[256,256]{1,0:T(8,128)(2,1)}, u32[]{:S(2)}) copy-start(bf16[256,256]{1,0:T(8,128)(2,1)} %constant.16.clone.half) | copy-start | bytes 393220
  0.6 16.3 %copy-start = (bf16[128,1024]{1,0:T(8,128)(2,1)S(1)}, bf16[128,1024]{1,0:T(8,128)(2,1)}, u32[]{:S(2)}) copy-start(bf16[128,1024]{1,0:T(8,128)(2,1)} %key_se.3) | copy-start | bytes 786436
  0.7 16.3 %copy-start.1 = (bf16[128,1024]{1,0:T(8,128)(2,1)S(1)}, bf16[128,1024]{1,0:T(8,128)(2,1)}, u32[]{:S(2)}) copy-start(bf16[128,1024]{1,0:T(8,128)(2,1)} %value.5) | copy-start | bytes 786436
  1.8 17.1 %copy-start.14 = (bf16[1024]{0:T(1024)(128)(2,1)S(1)}, bf16[1024]{0:T(1024)(128)(2,1)}, u32[]{:S(2)}) copy-start(bf16[1024]{0:T(1024)(128)(2,1)} %param.20) | copy-start | bytes 6148
  1.8 22.0 %collective-permute-start = (bf16[128,1024]{1,0:T(8,128)(2,1)S(1)}, bf16[128,1024]{1,0:T(8,128)(2,1)S(1)}, u32[]{:S(2)}, u32[]{:S(2)}) collective-permute-start(bf16[128,1024]{1,0:T(8,128)(2,1)S(1)} %multiply_convert_fusion.grad), channel_id=1, source_target_pairs={{8,0},{16,8},{24,16},{32,24},{40,32},{48,40},{56,48},{64,56},{72,6... | collective-permute-start | bytes 786440 | tf_op jit(solution)/shard_map/ppermute | solution.py:214
  17.0 5.8 %collective-permute-start.1 = (bf16[16,1024]{1,0:T(8,128)(2,1)S(1)}, bf16[16,1024]{1,0:T(8,128)(2,1)S(1)}, u32[]{:S(2)}, u32[]{:S(2)}) collective-permute-start(bf16[16,1024]{1,0:T(8,128)(2,1)S(1)} %multiply_convert_fusion.1), channel_id=1, source_target_pairs={{0,8},{8,16},{16,24},{24,32},{32,40},{40,48},{48,56},{56,64},{64,7... | collective-permute-start | bytes 98312 | tf_op jit(solution)/shard_map/ppermute | solution.py:214
  18.9 1.0 copy-start.11
  19.9 2.9 %copy-start.2 = (bf16[128,1024]{1,0:T(8,128)(2,1)S(1)}, bf16[128,1024]{1,0:T(8,128)(2,1)}, u32[]{:S(2)}) copy-start(bf16[128,1024]{1,0:T(8,128)(2,1)} %query_se.1) | copy-start | bytes 786436
  19.9 2.9 %copy-start.10 = (bf16[7,1024]{1,0:T(8,128)(2,1)S(1)}, bf16[7,1024]{1,0:T(8,128)(2,1)}, u32[]{:S(2)}) copy-start(bf16[7,1024]{1,0:T(8,128)(2,1)} %taps_se.1) | copy-start | bytes 43012
  20.3 3.5 %copy-start.4 = (bf16[128,1024]{1,0:T(8,128)(2,1)S(1)}, bf16[128,1024]{1,0:T(8,128)(2,1)}, u32[]{:S(2)}) copy-start(bf16[128,1024]{1,0:T(8,128)(2,1)} %key_mr.1) | copy-start | bytes 786436
  20.3 3.5 %copy-start.5 = (bf16[128,768]{1,0:T(8,128)(2,1)S(1)}, bf16[128,768]{1,0:T(8,128)(2,1)}, u32[]{:S(2)}) copy-start(bf16[128,768]{1,0:T(8,128)(2,1)} %constant.18.clone.back) | copy-start | bytes 589828
  20.4 3.5 %copy-start.9 = (bf16[256,256]{1,0:T(8,128)(2,1)S(1)}, bf16[256,256]{1,0:T(8,128)(2,1)}, u32[]{:S(2)}) copy-start(bf16[256,256]{1,0:T(8,128)(2,1)} %constant.17.clone.later) | copy-start | bytes 393220
  39.1 29.1 %all-to-all-start.1 = ((bf16[64,9,2,128]{3,2,1,0:T(2,128)(2,1)}), bf16[64,9,2,128]{3,2,1,0:T(2,128)(2,1)S(1)}, u32[]{:S(2)}, u32[]{:S(2)}) async-start(bf16[64,9,2,128]{3,2,1,0:T(2,128)(2,1)} %fusion), calls=%async_computation.1 | async-start | bytes 589824 | tf_op jit(solution)/shard_map/all_to_all | solution.py:225
  53.3 20.1 %collective-permute-start.2 = (bf16[128,1024]{1,0:T(8,128)(2,1)S(1)}, bf16[128,1024]{1,0:T(8,128)(2,1)S(1)}, u32[]{:S(2)}, u32[]{:S(2)}) collective-permute-start(bf16[128,1024]{1,0:T(8,128)(2,1)S(1)} %get-tuple-element.37.prod_mr), channel_id=1, source_target_pairs={{0,8},{8,16},{16,24},{24,32},{32,40},{40,48},{48,56},{56,64},{64,7... | collective-permute-start | bytes 786440 | tf_op jit(solution)/shard_map/ppermute | solution.py:214
  56.7 16.1 %collective-permute-start.3 = (bf16[16,1024]{1,0:T(8,128)(2,1)S(1)}, bf16[16,1024]{1,0:T(8,128)(2,1)S(1)}, u32[]{:S(2)}, u32[]{:S(2)}) collective-permute-start(bf16[16,1024]{1,0:T(8,128)(2,1)S(1)} %get-tuple-element.39), channel_id=1, source_target_pairs={{8,0},{16,8},{24,16},{32,24},{40,32},{48,40},{56,48},{64,56},{72,6... | collective-permute-start | bytes 98312 | tf_op jit(solution)/shard_map/ppermute | solution.py:214
  68.5 5.9 %copy-start.12 = (f32[9,2,128]{2,1,0:T(2,128)}, f32[9,2,128]{2,1,0:T(2,128)S(1)}, u32[]{:S(2)}) copy-start(f32[9,2,128]{2,1,0:T(2,128)S(1)} %convert_reduce_fusion.part) | copy-start | bytes 27652
  68.5 5.9 %collective-permute-start.4 = (f32[9,2,128]{2,1,0:T(2,128)S(1)}, f32[9,2,128]{2,1,0:T(2,128)S(1)}, u32[]{:S(2)}, u32[]{:S(2)}) collective-permute-start(f32[9,2,128]{2,1,0:T(2,128)S(1)} %convert_reduce_fusion.part), channel_id=1, source_target_pairs={{0,512},{8,520},{16,528},{24,536},{32,544},{40,552},{48,560},{56,5... | collective-permute-start | bytes 27656 | tf_op jit(solution)/shard_map/ppermute | solution.py:227
  74.4 0.6 copy-start.13
  76.3 7.8 %copy-start.7 = (bf16[128,768]{1,0:T(8,128)(2,1)S(1)}, bf16[128,768]{1,0:T(8,128)(2,1)}, u32[]{:S(2)}) copy-start(bf16[128,768]{1,0:T(8,128)(2,1)} %constant.19.clone.back) | copy-start | bytes 589828
  77.9 6.2 %copy-start.3 = (bf16[128,1024]{1,0:T(8,128)(2,1)S(1)}, bf16[128,1024]{1,0:T(8,128)(2,1)}, u32[]{:S(2)}) copy-start(bf16[128,1024]{1,0:T(8,128)(2,1)} %out_grad.1) | copy-start | bytes 786436
  77.9 6.2 %copy-start.6 = (bf16[256,512]{1,0:T(8,128)(2,1)S(1)}, bf16[256,512]{1,0:T(8,128)(2,1)}, u32[]{:S(2)}) copy-start(bf16[256,512]{1,0:T(8,128)(2,1)} %constant.15.clone.whole) | copy-start | bytes 786436
  77.9 19.6 %all-to-all-start.2 = ((bf16[64,9,2,128]{3,2,1,0:T(2,128)(2,1)}), bf16[64,9,2,128]{3,2,1,0:T(2,128)(2,1)S(1)}, u32[]{:S(2)}, u32[]{:S(2)}) async-start(bf16[64,9,2,128]{3,2,1,0:T(2,128)(2,1)} %broadcast_in_dim.2), calls=%async_computation.2 | async-start | bytes 589824 | tf_op jit(solution)/shard_map/all_to_all | solution.py:233

commit v6 on v5

--- a/solution.py
+++ b/solution.py
@@ -228,6 +228,7 @@
     total = pl.pallas_call(
         plane_kernel,
         out_shape=jax.ShapeDtypeStruct(part.shape, BF16),
+        compiler_params=pltpu.CompilerParams(vmem_limit_bytes=2 * 1024 * 1024),
     )(part, other, *[rim[:HALO, :128] for rim in rims])
     spread = jnp.broadcast_to(total[None], (plane,) + total.shape)
     back = lax.all_to_all(spread, "ctx", 0, 0, axis_index_groups=planes, tiled=True)
@@ -235,6 +236,7 @@
     return pl.pallas_call(
         unpack_kernel,
         out_shape=[jax.ShapeDtypeStruct(shape, F32) for shape in (mr_shape, se_shape, (1, cols))],
+        compiler_params=pltpu.CompilerParams(vmem_limit_bytes=6 * 1024 * 1024),
     )(back[:, :8].reshape(tiles.shape), back[:, 8, 0].astype(F32).reshape(-1, 8, 128))
 
 

time: 101 us -> 96.4 us (0.954)
  local copies, waits for them, and re-layouts: 5.3 us -> 2.1 us
  Pallas kernels: 9.72 us -> 7.45 us
  waiting for transfers between devices: 22.9 us -> 24.1 us
    pallas_call x1, Pallas kernels: 1.34 us -> 0.01 us  [filter_totals(): pl.pallas_call(plane_kernel, out_shape=jax.ShapeDtypeStruct(part.shape, B...]
    slice x2, local copies, waits for them, and re-layouts: 1.19 us -> 0.01 us  [filter_totals(): rim[:HALO, :128]]
    ppermute x1, waiting for transfers between devices: 0.42 us -> 1.58 us  [filter_totals(): other = lax.ppermute(part, 'ctx', [(i, (i + plane) % n) for i in range(n)])]
  transfers between devices with their start and end apart: 7 -> 7, of which waited for: 4 -> 4; matrix products, arithmetic and copies ran while one was open for 1% -> 0% of each run, Pallas kernels for 4% -> 4%
where the time goes in v6:
time: 96.4 us; the launch traced here: 95.9 us
  starting transfers between devices  47.5 us (49%)
  waiting for transfers between devices  24.1 us (25%)
  blocking collectives  11.4 us (12%)
  Pallas kernels  7.45 us (8%)
  other arithmetic  2.46 us (3%)
  local copies, waits for them, and re-layouts  2.1 us (2%)
    ppermute x4, starting transfers between devices, shifted(): return lax.ppermute(block, axis, route)  22.9 us
    all_to_all x1, starting transfers between devices, filter_totals(): lax.all_to_all(packed, 'ctx', 0, 0, axis_index_groups=planes, tiled=True)  14.2 us
    all_to_all x1, blocking collectives, shards(): stats = lax.all_to_all(stats, 'tp', 0, 0, tiled=True)  11.4 us
    all_to_all x1, waiting for transfers between devices, filter_totals(): lax.all_to_all(spread, 'ctx', 0, 0, axis_index_groups=planes, tiled=True)  11 us
    all_to_all x1, waiting for transfers between devices, filter_totals(): lax.all_to_all(packed, 'ctx', 0, 0, axis_index_groups=planes, tiled=True)  9.03 us
    all_to_all x1, starting transfers between devices, filter_totals(): lax.all_to_all(spread, 'ctx', 0, 0, axis_index_groups=planes, tiled=True)  6.16 us
    ppermute x1, starting transfers between devices, filter_totals(): other = lax.ppermute(part, 'ctx', [(i, (i + plane) % n) for i in range(n)])  4.28 us
    ppermute x4, waiting for transfers between devices, shifted(): return lax.ppermute(block, axis, route)  2.42 us
  transfers between devices with their start and end apart: 7, of which 4 were waited for; matrix products, arithmetic and copies ran while one was open for 0% of the time, Pallas kernels for 4%

profile of v6, /device:TPU:2, one launch (start us, length us, event | category | flops | bytes accessed | tf_op | source)
XLA Modules:
  0.0 95.9 jit_solution(13863219026151888950)
XLA Ops:
  0.6 0.0 copy-start.8
  0.6 0.0 copy-start
  0.7 0.0 copy-start.1
  0.7 1.2 %multiply_convert_fusion.grad = bf16[128,1024]{1,0:T(8,128)(2,1)S(1)} fusion(bf16[128,1024]{1,0:T(8,128)(2,1)} %param.18, bf16[128,1024]{1,0:T(8,128)(2,1)} %out_grad.1), kind=kLoop, calls=%fused_computation.2 | loop fusion | flops 524288 | bytes 786432 | tf_op jit(solution)/shard_map/convert_element_type | solution.py:252
  1.8 0.0 copy-start.12
  1.8 15.1 %collective-permute-start = (bf16[128,1024]{1,0:T(8,128)(2,1)S(1)}, bf16[128,1024]{1,0:T(8,128)(2,1)S(1)}, u32[]{:S(2)}, u32[]{:S(2)}) collective-permute-start(bf16[128,1024]{1,0:T(8,128)(2,1)S(1)} %multiply_convert_fusion.grad), channel_id=1, source_target_pairs={{8,0},{16,8},{24,16},{32,24},{40,32},{48,40},{56,48},{64,56},{72,6... | collective-permute-start | bytes 786440 | tf_op jit(solution)/shard_map/ppermute | solution.py:214
  16.9 0.0 copy-done
  17.0 0.0 copy-done.1
  17.0 1.9 %collective-permute-start.1 = (bf16[16,1024]{1,0:T(8,128)(2,1)S(1)}, bf16[16,1024]{1,0:T(8,128)(2,1)S(1)}, u32[]{:S(2)}, u32[]{:S(2)}) collective-permute-start(bf16[16,1024]{1,0:T(8,128)(2,1)S(1)} %multiply_convert_fusion.1), channel_id=1, source_target_pairs={{0,8},{8,16},{16,24},{24,32},{32,40},{40,48},{48,56},{56,64},{64,7... | collective-permute-start | bytes 98312 | tf_op jit(solution)/shard_map/ppermute | solution.py:214
  18.9 0.0 copy-done.12
  18.9 0.0 copy-done.8
  18.9 0.0 copy-start.11
  19.0 0.9 copy-done.11
  19.9 0.0 copy-start.2
  19.9 0.0 copy-start.10
  19.9 0.4 shard_map.197
  20.3 0.0 copy-start.4
  20.3 0.0 copy-start.5
  20.4 0.0 copy-start.9
  20.4 2.4 %collective-permute-done.1.rim = bf16[16,1024]{1,0:T(8,128)(2,1)S(1)} collective-permute-done((bf16[16,1024]{1,0:T(8,128)(2,1)S(1)}, bf16[16,1024]{1,0:T(8,128)(2,1)S(1)}, u32[]{:S(2)}, u32[]{:S(2)}) %collective-permute-start.1) | collective-permute-done | bytes 32800 | tf_op jit(solution)/shard_map/ppermute | solution.py:214
  22.8 0.0 copy-done.2
  22.8 0.0 copy-done.10
  22.8 1.0 %shard_map.198 = (f32[128,1024]{1,0:T(8,128)S(1)}, f32[128,1024]{1,0:T(8,128)S(1)}, f32[128,128]{1,0:T(8,128)S(1)}) custom-call(bf16[128,1024]{1,0:T(8,128)(2,1)S(1)} %copy-done, bf16[128,1024]{1,0:T(8,128)(2,1)S(1)} %copy-done.1, bf16[128,1024]{1,0:T(8,128)(2,1)S(1)} %copy-done.2, bf16[16,1024]{1,0:T(8,128)(2,1)S(1)} %collective-permute-done.1.rim, ...), custom_call_target="tpu_custom_call" | custom-call | flops 2359296 | bytes 1835008 | tf_op jit(solution)/shard_map/pallas_call | solution.py:267
  23.8 0.0 collective-permute-done.rim
  23.8 0.0 copy-done.4
  23.8 0.0 copy-done.5
  23.8 0.0 copy-done.9
  23.9 0.9 shard_map.199
  24.7 11.4 %all_to_all.15.stats = f32[8,8,128]{2,1,0:T(8,128)S(1)} all-to-all(f32[8,8,128]{2,1,0:T(8,128)S(1)} %get-tuple-element.33), channel_id=1, replica_groups=mesh['ctx'=128,'tp'=8] {'tp'}, dimensions={0} | all-to-all | bytes 65536 | tf_op jit(solution)/shard_map/all_to_all | solution.py:288
  36.2 1.9 %shard_map.200 = (bf16[128,1024]{1,0:T(8,128)(2,1)}, bf16[128,1024]{1,0:T(8,128)(2,1)}, bf16[128,1024]{1,0:T(8,128)(2,1)S(1)}, bf16[128,1024]{1,0:T(8,128)(2,1)S...) custom-call(f32[8,8,128]{2,1,0:T(8,128)S(1)} %all_to_all.15.stats, ...), custom_call_target="tpu_custom_call" | custom-call | flops 262144000 | bytes 5242880 | tf_op jit(solution)/shard_map/pallas_call | solution.py:292
  38.1 1.0 %fusion = bf16[64,9,2,128]{3,2,1,0:T(2,128)(2,1)} fusion(bf16[64,1,1,128]{3,2,1,0:T(2,128)(2,1)S(1)} %copy.24, bf16[64,8,2,128]{3,2,1,0:T(2,128)(2,1)S(1)} %bitcast.11), kind=kLoop, calls=%fused_computation.3 | loop fusion | flops 884736 | bytes 573440 | tf_op jit(solution)/shard_map/concatenate | solution.py:224
  39.1 14.2 %all-to-all-start.1 = ((bf16[64,9,2,128]{3,2,1,0:T(2,128)(2,1)}), bf16[64,9,2,128]{3,2,1,0:T(2,128)(2,1)S(1)}, u32[]{:S(2)}, u32[]{:S(2)}) async-start(bf16[64,9,2,128]{3,2,1,0:T(2,128)(2,1)} %fusion), calls=%async_computation.1 | async-start | bytes 589824 | tf_op jit(solution)/shard_map/all_to_all | solution.py:225
  53.3 3.4 %collective-permute-start.2 = (bf16[128,1024]{1,0:T(8,128)(2,1)S(1)}, bf16[128,1024]{1,0:T(8,128)(2,1)S(1)}, u32[]{:S(2)}, u32[]{:S(2)}) collective-permute-start(bf16[128,1024]{1,0:T(8,128)(2,1)S(1)} %get-tuple-element.37.prod_mr), channel_id=1, source_target_pairs={{0,8},{8,16},{16,24},{24,32},{32,40},{40,48},{48,56},{56,64},{64,7... | collective-permute-start | bytes 786440 | tf_op jit(solution)/shard_map/ppermute | solution.py:214
  56.7 2.5 %collective-permute-start.3 = (bf16[16,1024]{1,0:T(8,128)(2,1)S(1)}, bf16[16,1024]{1,0:T(8,128)(2,1)S(1)}, u32[]{:S(2)}, u32[]{:S(2)}) collective-permute-start(bf16[16,1024]{1,0:T(8,128)(2,1)S(1)} %get-tuple-element.39), channel_id=1, source_target_pairs={{8,0},{16,8},{24,16},{32,24},{40,32},{48,40},{56,48},{64,56},{72,6... | collective-permute-start | bytes 98312 | tf_op jit(solution)/shard_map/ppermute | solution.py:214
  59.2 9.0 %all-to-all-done.1 = bf16[64,9,2,128]{3,2,1,0:T(2,128)(2,1)S(1)} async-done(((bf16[64,9,2,128]{3,2,1,0:T(2,128)(2,1)}), bf16[64,9,2,128]{3,2,1,0:T(2,128)(2,1)S(1)}, u32[]{:S(2)}, u32[]{:S(2)}) %all-to-all-start.1) | async-done | bytes 294944 | tf_op jit(solution)/shard_map/all_to_all | solution.py:225
  68.2 0.3 convert_reduce_fusion.part
  68.5 4.3 %collective-permute-start.4 = (f32[9,2,128]{2,1,0:T(2,128)S(1)}, f32[9,2,128]{2,1,0:T(2,128)S(1)}, u32[]{:S(2)}, u32[]{:S(2)}) collective-permute-start(f32[9,2,128]{2,1,0:T(2,128)S(1)} %convert_reduce_fusion.part), channel_id=1, source_target_pairs={{0,512},{8,520},{16,528},{24,536},{32,544},{40,552},{48,560},{56,5... | collective-permute-start | bytes 27656 | tf_op jit(solution)/shard_map/ppermute | solution.py:227
  72.7 0.0 collective-permute-done.3.rim_se
  72.8 0.0 collective-permute-done.2.rim_mr
  72.8 1.6 %collective-permute-done.4.other = f32[9,2,128]{2,1,0:T(2,128)S(1)} collective-permute-done((f32[9,2,128]{2,1,0:T(2,128)S(1)}, f32[9,2,128]{2,1,0:T(2,128)S(1)}, u32[]{:S(2)}, u32[]{:S(2)}) %collective-permute-start.4) | collective-permute-done | bytes 9248 | tf_op jit(solution)/shard_map/ppermute | solution.py:227
  74.4 0.0 copy-start.7
  74.4 0.9 broadcast_in_dim.2
  75.3 0.0 copy-start.3
  75.3 0.0 copy-start.6
  75.3 6.2 %all-to-all-start.2 = ((bf16[64,9,2,128]{3,2,1,0:T(2,128)(2,1)}), bf16[64,9,2,128]{3,2,1,0:T(2,128)(2,1)S(1)}, u32[]{:S(2)}, u32[]{:S(2)}) async-start(bf16[64,9,2,128]{3,2,1,0:T(2,128)(2,1)} %broadcast_in_dim.2), calls=%async_computation.2 | async-start | bytes 589824 | tf_op jit(solution)/shard_map/all_to_all | solution.py:234
  81.4 0.0 copy-done.7
  81.4 0.0 copy-done.3
  81.4 0.0 copy-done.6
  81.5 2.4 %shard_map.201 = (bf16[128,1024]{1,0:T(8,128)(2,1)}, bf16[128,1024]{1,0:T(8,128)(2,1)}, bf16[128,1024]{1,0:T(8,128)(2,1)}) custom-call(bf16[128,1024]{1,0:T(8,128)(2,1)S(1)} %get-tuple-element.37.prod_mr, bf16[128,1024]{1,0:T(8,128)(2,1)S(1)} %collective-permute-done.2.rim_mr, bf16[128,1024]{1,0:T(8,128)(2,1)S(1)} %copy-done.3, ...), custom_call_target="tpu_custom_call" | custom-call | flops 393216000 | bytes 2621440 | tf_op jit(solution)/shard_map/pallas_call | solution.py:312
  83.8 11.0 %all-to-all-done.2 = bf16[64,9,2,128]{3,2,1,0:T(2,128)(2,1)S(1)} async-done(((bf16[64,9,2,128]{3,2,1,0:T(2,128)(2,1)}), bf16[64,9,2,128]{3,2,1,0:T(2,128)(2,1)S(1)}, u32[]{:S(2)}, u32[]{:S(2)}) %all-to-all-start.2) | async-done | bytes 294944 | tf_op jit(solution)/shard_map/all_to_all | solution.py:234
  94.9 0.2 slice.26
  95.1 0.9 shard_map.203
  (8 shorter events, 0.1 us)
Async XLA Ops:
  0.6 18.3 %copy-start.8 = (bf16[256,256]{1,0:T(8,128)(2,1)S(1)}, bf16[256,256]{1,0:T(8,128)(2,1)}, u32[]{:S(2)}) copy-start(bf16[256,256]{1,0:T(8,128)(2,1)} %constant.16.clone.half) | copy-start | bytes 393220
  0.6 16.3 %copy-start = (bf16[128,1024]{1,0:T(8,128)(2,1)S(1)}, bf16[128,1024]{1,0:T(8,128)(2,1)}, u32[]{:S(2)}) copy-start(bf16[128,1024]{1,0:T(8,128)(2,1)} %key_se.3) | copy-start | bytes 786436
  0.7 16.3 %copy-start.1 = (bf16[128,1024]{1,0:T(8,128)(2,1)S(1)}, bf16[128,1024]{1,0:T(8,128)(2,1)}, u32[]{:S(2)}) copy-start(bf16[128,1024]{1,0:T(8,128)(2,1)} %value.5) | copy-start | bytes 786436
  1.8 17.1 %copy-start.12 = (bf16[1024]{0:T(1024)(128)(2,1)S(1)}, bf16[1024]{0:T(1024)(128)(2,1)}, u32[]{:S(2)}) copy-start(bf16[1024]{0:T(1024)(128)(2,1)} %param.20) | copy-start | bytes 6148
  1.8 22.0 %collective-permute-start = (bf16[128,1024]{1,0:T(8,128)(2,1)S(1)}, bf16[128,1024]{1,0:T(8,128)(2,1)S(1)}, u32[]{:S(2)}, u32[]{:S(2)}) collective-permute-start(bf16[128,1024]{1,0:T(8,128)(2,1)S(1)} %multiply_convert_fusion.grad), channel_id=1, source_target_pairs={{8,0},{16,8},{24,16},{32,24},{40,32},{48,40},{56,48},{64,56},{72,6... | collective-permute-start | bytes 786440 | tf_op jit(solution)/shard_map/ppermute | solution.py:214
  17.0 5.8 %collective-permute-start.1 = (bf16[16,1024]{1,0:T(8,128)(2,1)S(1)}, bf16[16,1024]{1,0:T(8,128)(2,1)S(1)}, u32[]{:S(2)}, u32[]{:S(2)}) collective-permute-start(bf16[16,1024]{1,0:T(8,128)(2,1)S(1)} %multiply_convert_fusion.1), channel_id=1, source_target_pairs={{0,8},{8,16},{16,24},{24,32},{32,40},{40,48},{48,56},{56,64},{64,7... | collective-permute-start | bytes 98312 | tf_op jit(solution)/shard_map/ppermute | solution.py:214
  18.9 1.0 copy-start.11
  19.9 2.9 %copy-start.2 = (bf16[128,1024]{1,0:T(8,128)(2,1)S(1)}, bf16[128,1024]{1,0:T(8,128)(2,1)}, u32[]{:S(2)}) copy-start(bf16[128,1024]{1,0:T(8,128)(2,1)} %query_se.1) | copy-start | bytes 786436
  19.9 2.9 %copy-start.10 = (bf16[7,1024]{1,0:T(8,128)(2,1)S(1)}, bf16[7,1024]{1,0:T(8,128)(2,1)}, u32[]{:S(2)}) copy-start(bf16[7,1024]{1,0:T(8,128)(2,1)} %taps_se.1) | copy-start | bytes 43012
  20.3 3.5 %copy-start.4 = (bf16[128,1024]{1,0:T(8,128)(2,1)S(1)}, bf16[128,1024]{1,0:T(8,128)(2,1)}, u32[]{:S(2)}) copy-start(bf16[128,1024]{1,0:T(8,128)(2,1)} %key_mr.1) | copy-start | bytes 786436
  20.3 3.5 %copy-start.5 = (bf16[128,768]{1,0:T(8,128)(2,1)S(1)}, bf16[128,768]{1,0:T(8,128)(2,1)}, u32[]{:S(2)}) copy-start(bf16[128,768]{1,0:T(8,128)(2,1)} %constant.18.clone.back) | copy-start | bytes 589828
  20.4 3.5 %copy-start.9 = (bf16[256,256]{1,0:T(8,128)(2,1)S(1)}, bf16[256,256]{1,0:T(8,128)(2,1)}, u32[]{:S(2)}) copy-start(bf16[256,256]{1,0:T(8,128)(2,1)} %constant.17.clone.later) | copy-start | bytes 393220
  39.1 29.1 %all-to-all-start.1 = ((bf16[64,9,2,128]{3,2,1,0:T(2,128)(2,1)}), bf16[64,9,2,128]{3,2,1,0:T(2,128)(2,1)S(1)}, u32[]{:S(2)}, u32[]{:S(2)}) async-start(bf16[64,9,2,128]{3,2,1,0:T(2,128)(2,1)} %fusion), calls=%async_computation.1 | async-start | bytes 589824 | tf_op jit(solution)/shard_map/all_to_all | solution.py:225
  53.3 19.5 %collective-permute-start.2 = (bf16[128,1024]{1,0:T(8,128)(2,1)S(1)}, bf16[128,1024]{1,0:T(8,128)(2,1)S(1)}, u32[]{:S(2)}, u32[]{:S(2)}) collective-permute-start(bf16[128,1024]{1,0:T(8,128)(2,1)S(1)} %get-tuple-element.37.prod_mr), channel_id=1, source_target_pairs={{0,8},{8,16},{16,24},{24,32},{32,40},{40,48},{48,56},{56,64},{64,7... | collective-permute-start | bytes 786440 | tf_op jit(solution)/shard_map/ppermute | solution.py:214
  56.7 16.1 %collective-permute-start.3 = (bf16[16,1024]{1,0:T(8,128)(2,1)S(1)}, bf16[16,1024]{1,0:T(8,128)(2,1)S(1)}, u32[]{:S(2)}, u32[]{:S(2)}) collective-permute-start(bf16[16,1024]{1,0:T(8,128)(2,1)S(1)} %get-tuple-element.39), channel_id=1, source_target_pairs={{8,0},{16,8},{24,16},{32,24},{40,32},{48,40},{56,48},{64,56},{72,6... | collective-permute-start | bytes 98312 | tf_op jit(solution)/shard_map/ppermute | solution.py:214
  68.5 5.9 %collective-permute-start.4 = (f32[9,2,128]{2,1,0:T(2,128)S(1)}, f32[9,2,128]{2,1,0:T(2,128)S(1)}, u32[]{:S(2)}, u32[]{:S(2)}) collective-permute-start(f32[9,2,128]{2,1,0:T(2,128)S(1)} %convert_reduce_fusion.part), channel_id=1, source_target_pairs={{0,512},{8,520},{16,528},{24,536},{32,544},{40,552},{48,560},{56,5... | collective-permute-start | bytes 27656 | tf_op jit(solution)/shard_map/ppermute | solution.py:227
  74.4 7.1 %copy-start.7 = (bf16[128,768]{1,0:T(8,128)(2,1)S(1)}, bf16[128,768]{1,0:T(8,128)(2,1)}, u32[]{:S(2)}) copy-start(bf16[128,768]{1,0:T(8,128)(2,1)} %constant.19.clone.back) | copy-start | bytes 589828
  75.3 6.2 %copy-start.3 = (bf16[128,1024]{1,0:T(8,128)(2,1)S(1)}, bf16[128,1024]{1,0:T(8,128)(2,1)}, u32[]{:S(2)}) copy-start(bf16[128,1024]{1,0:T(8,128)(2,1)} %out_grad.1) | copy-start | bytes 786436
  75.3 6.2 %copy-start.6 = (bf16[256,512]{1,0:T(8,128)(2,1)S(1)}, bf16[256,512]{1,0:T(8,128)(2,1)}, u32[]{:S(2)}) copy-start(bf16[256,512]{1,0:T(8,128)(2,1)} %constant.15.clone.whole) | copy-start | bytes 786436
  75.3 19.6 %all-to-all-start.2 = ((bf16[64,9,2,128]{3,2,1,0:T(2,128)(2,1)}), bf16[64,9,2,128]{3,2,1,0:T(2,128)(2,1)S(1)}, u32[]{:S(2)}, u32[]{:S(2)}) async-start(bf16[64,9,2,128]{3,2,1,0:T(2,128)(2,1)} %broadcast_in_dim.2), calls=%async_computation.2 | async-start | bytes 589824 | tf_op jit(solution)/shard_map/all_to_all | solution.py:234
